TPU v7x, 32 devices: a whole 2x2x4 slice. The times are simulated.
32 devices in a mesh: batch: 4 (over y, x), seq: 8 (over z, core).
Axes of the slice: x: 2, y: 2, z: 4, core: 2. Of those that a mesh axis runs over, the one named last changes fastest.
Arguments:
- tokens: bfloat16 [16, 1024, 1024], P('batch', 'seq'), may hold values from -6 to 6
- cotangent: bfloat16 [16, 1024, 1024], P('batch', 'seq'), may hold values from -6 to 6
- prenorm_gain: float32 [1024], replicated, may hold values from 0.25 to 1.75
- inproj_weight: bfloat16 [1024, 4384], P(('batch', 'seq')), may hold values from -0.1875 to 0.1875
- conv_taps: float32 [4, 2304], replicated, may hold values from -3 to 3
- conv_bias: float32 [2304], replicated, may hold values from -0.5 to 0.5
- step_bias: float32 [32], replicated, may hold values from -5.5 to -2.5
- decay_log: float32 [32], replicated, may hold values from 0 to 2.77
- skip_weight: float32 [32], replicated, may hold values from 0.5 to 1.5
- postnorm_gain: float32 [2048], replicated, may hold values from 0.25 to 1.75
- outproj_weight: bfloat16 [1024, 2048], P(('batch', 'seq')), may hold values from -0.125 to 0.125
Outputs:
- mixed: bfloat16 [16, 1024, 1024], P('batch', 'seq')
- input_grad: float32 [16, 1024, 1024], P('batch', 'seq')
- prenorm_grad: float32 [1024], replicated
- inproj_grad: float32 [1024, 4384], P(('batch', 'seq'))
- taps_grad: float32 [4, 2304], replicated
- bias_grad: float32 [2304], replicated
- step_grad: float32 [32], replicated
- decay_grad: float32 [32], replicated
- skip_grad: float32 [32], replicated
- postnorm_grad: float32 [2048], replicated
- outproj_grad: float32 [1024, 2048], P(('batch', 'seq'))
All inputs are finite; a program needn't handle non-finite values.
Results may differ from a plain program's by a relative error of at most 0.012.
The roundings to bfloat16 on the way count: a program that leaves them out, or rounds other values in their place, can miss the bound.
Values may be sent and summed in bfloat16 or wider, within the bound.
A program may use at most 256 MiB of HBM per device.

v0:
```python
import jax
import jax.numpy as jnp
from jax import lax
from jax.sharding import PartitionSpec as P

HEADS = 32
HEADDIM = 64
STATE = 128
CONV = 4
BLOCK = 256
INNER = 2048
PROJ = 4384


EPS = 1e-05
HIGH = lax.Precision.HIGHEST


def causal_filter(values, taps, bias):
    length = values.shape[0]
    padded = jnp.concatenate(
        [jnp.zeros((taps.shape[0] - 1, values.shape[1]), jnp.float32), values], 0
    )
    total = jnp.zeros(values.shape, jnp.float32) + bias[None, :]
    for offset in range(taps.shape[0]):
        total = total + taps[offset][None, :] * padded[offset : offset + length]
    return total


def state_space(x_heads, dt_heads, b_rows, c_rows, decay_log, skip_weight, block):
    length, heads, width = x_heads.shape
    block_count = length // block
    rate = -jnp.exp(decay_log)
    x_blocks = x_heads.reshape(block_count, block, heads, width)
    a_blocks = (dt_heads * rate[None, :]).reshape(block_count, block, heads)
    dt_blocks = jnp.swapaxes(dt_heads.reshape(block_count, block, heads), 1, 2)
    b_blocks = b_rows.reshape(block_count, block, -1)
    c_blocks = c_rows.reshape(block_count, block, -1)
    row_ids = lax.broadcasted_iota(jnp.int32, (block, block), 0)
    col_ids = lax.broadcasted_iota(jnp.int32, (block, block), 1)
    lower = row_ids >= col_ids
    cum_decay = jnp.einsum("ij,cjh->chi", lower.astype(jnp.float32), a_blocks, precision=HIGH)
    scores = jnp.einsum("cin,cjn->cij", c_blocks, b_blocks, precision=HIGH)
    gap = cum_decay[:, :, :, None] - cum_decay[:, :, None, :]
    decay = jnp.where(lower, jnp.exp(jnp.where(lower, gap, 0.0)), 0.0)
    weights = decay * scores[:, None] * dt_blocks[:, :, None, :]
    y_diag = jnp.einsum("chij,cjhp->cihp", weights, x_blocks, precision=HIGH)
    to_end = jnp.exp(cum_decay[:, :, -1:] - cum_decay) * dt_blocks
    weighted_x = x_blocks * jnp.swapaxes(to_end, 1, 2)[..., None]
    block_state = jnp.einsum("cjn,cjhp->chnp", b_blocks, weighted_x, precision=HIGH)
    totals = cum_decay[:, :, -1]
    block_rows = lax.broadcasted_iota(jnp.int32, (block_count, block_count), 0)
    block_cols = lax.broadcasted_iota(jnp.int32, (block_count, block_count), 1)
    block_cum = jnp.einsum(
        "kg,gh->kh", (block_rows >= block_cols).astype(jnp.float32), totals, precision=HIGH
    )
    entering = block_cum - totals
    before = (block_cols < block_rows)[:, :, None]
    span = entering[:, None, :] - block_cum[None, :, :]
    carry = jnp.where(before, jnp.exp(jnp.where(before, span, 0.0)), 0.0)
    start_state = jnp.einsum("kgh,ghnp->khnp", carry, block_state, precision=HIGH)
    y_off = jnp.einsum("cin,chnp->cihp", c_blocks, start_state, precision=HIGH)
    y_off = y_off * jnp.swapaxes(jnp.exp(cum_decay), 1, 2)[..., None]
    result = y_diag + y_off + skip_weight[None, None, :, None] * x_blocks
    return result.reshape(length, heads, width)


def mixer_block(
    x_heads, step_heads, bc_all, taps_x, bias_x, taps_bc, bias_bc, step_part, decay_part, skip_part
):

    def single_row(row_args):
        x_row, step_row, bc_row = row_args
        length = x_row.shape[0]
        x_conv = jax.nn.silu(causal_filter(x_row, taps_x, bias_x))
        bc_conv = jax.nn.silu(causal_filter(bc_row, taps_bc, bias_bc))
        step_vals = jax.nn.softplus(step_row + step_part[None, :])
        result = state_space(
            x_conv.reshape(length, -1, HEADDIM),
            step_vals,
            bc_conv[:, :STATE],
            bc_conv[:, STATE:],
            decay_part,
            skip_part,
            BLOCK,
        )
        return result.reshape(length, -1)

    return lax.map(jax.checkpoint(single_row), (x_heads, step_heads, bc_all))


def prenorm(row, gain):
    return row * lax.rsqrt(jnp.mean(row * row, -1, keepdims=True) + EPS) * gain


def postnorm(y_tokens, gate, gain):
    gated = y_tokens * jax.nn.silu(gate)
    return gated * lax.rsqrt(jnp.mean(gated * gated, -1, keepdims=True) + EPS) * gain


def local(
    tokens,
    cotangent,
    prenorm_gain,
    inproj_weight,
    conv_taps,
    conv_bias,
    step_bias,
    decay_log,
    skip_weight,
    postnorm_gain,
    outproj_weight,
):
    seqs, seq_tok, width = tokens.shape
    rows = seqs * seq_tok
    group = lax.axis_size("seq")
    index = lax.axis_index("seq")
    contract_last = (((1,), (1,)), ((), ()))
    contract_first = (((0,), (0,)), ((), ()))
    token_f = tokens.astype(jnp.float32)
    normed_f, pre_back = jax.vjp(prenorm, token_f, prenorm_gain)
    normed = normed_f.astype(jnp.bfloat16).reshape(rows, width)
    part = normed
    proj = jnp.dot(
        part,
        lax.all_gather(inproj_weight, ("batch", "seq"), axis=0, tiled=True),
        preferred_element_type=jnp.float32,
    )
    gate = proj[:, :INNER].reshape(seqs, seq_tok, INNER)
    x_send = proj[:, INNER : 2 * INNER].astype(jnp.bfloat16).reshape(seqs, seq_tok, INNER)
    bc_send = (
        proj[:, 2 * INNER : 2 * INNER + 2 * STATE]
        .astype(jnp.bfloat16)
        .reshape(seqs, seq_tok, 2 * STATE)
    )
    step_send = proj[:, 2 * INNER + 2 * STATE :].astype(jnp.bfloat16).reshape(seqs, seq_tok, HEADS)
    head_group = HEADS // group
    x_heads, step_heads = (
        lax.all_to_all(x_send, "seq", split_axis=2, concat_axis=1, tiled=True),
        lax.all_to_all(step_send, "seq", split_axis=2, concat_axis=1, tiled=True),
    )
    bc_all = lax.all_gather(bc_send, "seq", axis=1, tiled=True)
    channels = head_group * HEADDIM
    first = index * channels
    head_first = index * head_group
    taps_x = lax.dynamic_slice_in_dim(conv_taps, first, channels, 1)
    bias_x = lax.dynamic_slice_in_dim(conv_bias, first, channels, 0)
    taps_bc = conv_taps[:, INNER:]
    bias_bc = conv_bias[INNER:]
    step_part = lax.dynamic_slice_in_dim(step_bias, head_first, head_group, 0)
    decay_part = lax.dynamic_slice_in_dim(decay_log, head_first, head_group, 0)
    skip_part = lax.dynamic_slice_in_dim(skip_weight, head_first, head_group, 0)
    mixed_heads, mix_back = jax.vjp(
        mixer_block,
        x_heads.astype(jnp.float32),
        step_heads.astype(jnp.float32),
        bc_all.astype(jnp.float32),
        taps_x,
        bias_x,
        taps_bc,
        bias_bc,
        step_part,
        decay_part,
        skip_part,
    )
    y_tokens = lax.all_to_all(
        mixed_heads.astype(jnp.bfloat16), "seq", split_axis=1, concat_axis=2, tiled=True
    )
    y_norm_f, post_back = jax.vjp(postnorm, y_tokens.astype(jnp.float32), gate, postnorm_gain)
    y_norm = y_norm_f.astype(jnp.bfloat16).reshape(rows, INNER)
    branch = lax.dot_general(
        y_norm,
        lax.all_gather(outproj_weight, ("batch", "seq"), axis=0, tiled=True),
        contract_last,
        preferred_element_type=jnp.float32,
    )
    mixed = (token_f + branch.reshape(seqs, seq_tok, width)).astype(jnp.bfloat16)
    upstream = cotangent.reshape(rows, width)
    part = upstream
    outproj_grad = lax.psum_scatter(
        lax.dot_general(part, y_norm, contract_first, preferred_element_type=jnp.float32),
        ("batch", "seq"),
        scatter_dimension=0,
        tiled=True,
    )
    part = upstream
    y_norm_grad = jnp.dot(
        part,
        lax.all_gather(outproj_weight, ("batch", "seq"), axis=0, tiled=True),
        preferred_element_type=jnp.float32,
    )
    y_grad, gate_grad, postnorm_part = post_back(y_norm_grad.reshape(seqs, seq_tok, INNER))
    y_grad_low = y_grad.astype(jnp.bfloat16)
    y_grad_heads = lax.all_to_all(y_grad_low, "seq", split_axis=2, concat_axis=1, tiled=True)
    (
        x_grad,
        step_grad_heads,
        bc_grad,
        taps_x_grad,
        bias_x_grad,
        taps_bc_grad,
        bias_bc_grad,
        step_part_grad,
        decay_part_grad,
        skip_part_grad,
    ) = mix_back(y_grad_heads.astype(jnp.float32))
    x_back, step_back = (
        lax.all_to_all(x_grad.astype(jnp.bfloat16), "seq", split_axis=1, concat_axis=2, tiled=True),
        lax.all_to_all(
            step_grad_heads.astype(jnp.bfloat16), "seq", split_axis=1, concat_axis=2, tiled=True
        ),
    )
    bc_back = lax.psum_scatter(
        bc_grad.astype(jnp.bfloat16), "seq", scatter_dimension=1, tiled=True
    ).astype(jnp.float32)
    proj_grad = jnp.concatenate(
        [gate_grad, x_back.astype(jnp.float32), bc_back, step_back.astype(jnp.float32)], 2
    )
    proj_grad = proj_grad.astype(jnp.bfloat16).reshape(rows, PROJ)
    part = normed
    inproj_grad = lax.psum_scatter(
        lax.dot_general(part, proj_grad, contract_first, preferred_element_type=jnp.float32),
        ("batch", "seq"),
        scatter_dimension=0,
        tiled=True,
    )
    normed_grad = lax.dot_general(
        proj_grad,
        lax.all_gather(inproj_weight, ("batch", "seq"), axis=0, tiled=True),
        contract_last,
        preferred_element_type=jnp.float32,
    )
    token_grad, prenorm_part = pre_back(normed_grad.reshape(seqs, seq_tok, width))
    input_grad = cotangent.astype(jnp.float32) + token_grad
    taps_full = jnp.concatenate(
        [
            lax.dynamic_update_slice(
                jnp.zeros((CONV, INNER), jnp.float32), taps_x_grad, (0, first)
            ),
            taps_bc_grad,
        ],
        1,
    )
    bias_full = jnp.concatenate(
        [
            lax.dynamic_update_slice(jnp.zeros((INNER,), jnp.float32), bias_x_grad, (first,)),
            bias_bc_grad,
        ],
        0,
    )
    step_full = lax.dynamic_update_slice(
        jnp.zeros((HEADS,), jnp.float32), step_part_grad, (head_first,)
    )
    decay_full = lax.dynamic_update_slice(
        jnp.zeros((HEADS,), jnp.float32), decay_part_grad, (head_first,)
    )
    skip_full = lax.dynamic_update_slice(
        jnp.zeros((HEADS,), jnp.float32), skip_part_grad, (head_first,)
    )
    summed = lax.psum(
        (prenorm_part, taps_full, bias_full, step_full, decay_full, skip_full, postnorm_part),
        ("batch", "seq"),
    )
    return (
        mixed,
        input_grad,
        summed[0],
        inproj_grad,
        summed[1],
        summed[2],
        summed[3],
        summed[4],
        summed[5],
        summed[6],
        outproj_grad,
    )


def solution(mesh):
    in_specs = (
        P("batch", "seq", None),
        P("batch", "seq", None),
        P(),
        P(("batch", "seq"), None),
        P(),
        P(),
        P(),
        P(),
        P(),
        P(),
        P(("batch", "seq"), None),
    )
    out_specs = (
        P("batch", "seq", None),
        P("batch", "seq", None),
        P(),
        P(("batch", "seq"), None),
        P(),
        P(),
        P(),
        P(),
        P(),
        P(),
        P(("batch", "seq"), None),
    )
    return jax.shard_map(local, mesh=mesh, in_specs=in_specs, out_specs=out_specs, check_vma=False)
```

profile of v0, /device:TPU:0, one launch (start us, length us, event | category | flops | bytes accessed | tf_op | source)
XLA Modules:
  0.0 1398.9 jit_solution(4105537451320410736)
XLA Ops:
  12.2 82.2 %all-gather.4.cloned.1.call-done = bf16[1024,4384]{1,0:T(8,128)(2,1)} async-done(((bf16[32,4384]{1,0:T(8,128)(2,1)}), bf16[1024,4384]{1,0:T(8,128)(2,1)}) %all-gather.4.cloned.1.call-update) | async-done | bytes 8978448 | tf_op jit(solution)/shard_map/all_gather | solution.py:126
  94.4 13.3 fusion.215
  127.4 58.7 %all-to-all-done = bf16[4,128,2048]{1,0,2:T(4,128)(2,1)S(1)} async-done(((bf16[4,128,2048]{1,0,2:T(4,128)(2,1)}), bf16[4,128,2048]{1,0,2:T(4,128)(2,1)S(1)}, u32[]{:S(2)}, u32[]{:S(2)}) %all-to-all-start) | async-done | bytes 2097184 | tf_op jit(solution)/shard_map/all_to_all | solution.py:139
  200.8 166.8 %while.47 = (s32[]{:T(128)}, bf16[4,1024,256]{2,0,1:T(4,128)(2,1)}, f32[1,256]{1,0:T(1,128)S(1)}, f32[4,1024,256]{1,2,0:T(8,128)}, f32[1,256]{1,0:T(1,128)S(1)},...) while((s32[]{:T(128)}, bf16[4,1024,256]{2,0,1:T(4,128)(2,1)}, ...), condition=%wide.region_2.3_spmd.clone.clone, body=%wide.region_1.2_spmd.clone.clone.sunk | while | flops 2045449216 | bytes 32320492 | solution.py:89
  221.2 21.4 %dynamic_update_slice.67 = bf16[4,1024,256]{2,0,1:T(4,128)(2,1)} dynamic-update-slice(bf16[4,1024,256]{2,0,1:T(4,128)(2,1)} %get-tuple-element.1553, bf16[1,1024,256]{2,0,1:T(2,128)(2,1)S(1)} %reshape.498, s32[]{:T(128)S(6)} %copy.476, s32[]{:T(128)} %constant.139.clone.1..sunk, s32[]{:T(128)} %constant.139.clone.1..sunk) | dynamic-update-slice | bytes 1048580 | tf_op jit(solution)/shard_map/jvp()/while/body/jit(dynamic_update_index_in_dim)/dynamic_update_slice | solution.py:89
  262.9 21.3 %dynamic_update_slice.67 = bf16[4,1024,256]{2,0,1:T(4,128)(2,1)} dynamic-update-slice(bf16[4,1024,256]{2,0,1:T(4,128)(2,1)} %get-tuple-element.1553, bf16[1,1024,256]{2,0,1:T(2,128)(2,1)S(1)} %reshape.498, s32[]{:T(128)S(6)} %copy.476, s32[]{:T(128)} %constant.139.clone.1..sunk, s32[]{:T(128)} %constant.139.clone.1..sunk) | dynamic-update-slice | bytes 1048580 | tf_op jit(solution)/shard_map/jvp()/while/body/jit(dynamic_update_index_in_dim)/dynamic_update_slice | solution.py:89
  304.6 21.3 %dynamic_update_slice.67 = bf16[4,1024,256]{2,0,1:T(4,128)(2,1)} dynamic-update-slice(bf16[4,1024,256]{2,0,1:T(4,128)(2,1)} %get-tuple-element.1553, bf16[1,1024,256]{2,0,1:T(2,128)(2,1)S(1)} %reshape.498, s32[]{:T(128)S(6)} %copy.476, s32[]{:T(128)} %constant.139.clone.1..sunk, s32[]{:T(128)} %constant.139.clone.1..sunk) | dynamic-update-slice | bytes 1048580 | tf_op jit(solution)/shard_map/jvp()/while/body/jit(dynamic_update_index_in_dim)/dynamic_update_slice | solution.py:89
  346.3 21.3 %dynamic_update_slice.67 = bf16[4,1024,256]{2,0,1:T(4,128)(2,1)} dynamic-update-slice(bf16[4,1024,256]{2,0,1:T(4,128)(2,1)} %get-tuple-element.1553, bf16[1,1024,256]{2,0,1:T(2,128)(2,1)S(1)} %reshape.498, s32[]{:T(128)S(6)} %copy.476, s32[]{:T(128)} %constant.139.clone.1..sunk, s32[]{:T(128)} %constant.139.clone.1..sunk) | dynamic-update-slice | bytes 1048580 | tf_op jit(solution)/shard_map/jvp()/while/body/jit(dynamic_update_index_in_dim)/dynamic_update_slice | solution.py:89
  386.6 33.7 %all-to-all-done.2 = bf16[4,1024,256]{2,0,1:T(4,128)(2,1)S(1)} async-done(((bf16[4,1024,256]{2,0,1:T(4,128)(2,1)}), bf16[4,1024,256]{2,0,1:T(4,128)(2,1)S(1)}, u32[]{:S(2)}, u32[]{:S(2)}) %all-to-all-start.2) | async-done | bytes 2097184 | tf_op jit(solution)/shard_map/all_to_all | solution.py:166
  439.5 10.0 multiply_reduce_fusion.14
  461.2 48.0 %all-to-all-done.3 = bf16[4,128,2048]{1,0,2:T(4,128)(2,1)S(1)} async-done(((bf16[4,128,2048]{1,0,2:T(4,128)(2,1)}), bf16[4,128,2048]{1,0,2:T(4,128)(2,1)S(1)}, u32[]{:S(2)}, u32[]{:S(2)}) %all-to-all-start.3) | async-done | bytes 2097184 | tf_op jit(solution)/shard_map/all_to_all | solution.py:194
  522.2 456.8 %while.48 = (s32[]{:T(128)}, f32[256]{0:T(256)S(1)}, f32[4,256]{1,0:T(4,128)S(1)}, f32[256]{0:T(256)S(1)}, f32[4,256]{1,0:T(4,128)S(1)}, /*index=5*/f32[4]{0:T(1...) while((s32[]{:T(128)}, f32[256]{0:T(256)S(1)}, ...), condition=%wide.region_29.30_spmd.clone, body=%wide.region_5.29_spmd.clone.sunk | while | flops 5323447296 | bytes 149996736 | solution.py:89
  608.5 21.4 %dynamic_update_slice.70 = bf16[4,1024,256]{2,0,1:T(4,128)(2,1)} dynamic-update-slice(bf16[4,1024,256]{2,0,1:T(4,128)(2,1)} %get-tuple-element.1630, bf16[1,1024,256]{2,0,1:T(2,128)(2,1)} %copy.468, s32[]{:T(128)S(6)} %sub.482, s32[]{:T(128)} %constant.139.clone.1..sunk.1, s32[]{:T(128)} %constant.139.clone.1..sunk.1) | dynamic-update-slice | bytes 1048580 | tf_op jit(solution)/shard_map/transpose(jvp())/while/body/jit(dynamic_update_index_in_dim)/dynamic_update_slice | solution.py:89
  721.3 21.4 %dynamic_update_slice.70 = bf16[4,1024,256]{2,0,1:T(4,128)(2,1)} dynamic-update-slice(bf16[4,1024,256]{2,0,1:T(4,128)(2,1)} %get-tuple-element.1630, bf16[1,1024,256]{2,0,1:T(2,128)(2,1)} %copy.468, s32[]{:T(128)S(6)} %sub.482, s32[]{:T(128)} %constant.139.clone.1..sunk.1, s32[]{:T(128)} %constant.139.clone.1..sunk.1) | dynamic-update-slice | bytes 1048580 | tf_op jit(solution)/shard_map/transpose(jvp())/while/body/jit(dynamic_update_index_in_dim)/dynamic_update_slice | solution.py:89
  790.6 8.6 fusion.372
  834.0 21.4 %dynamic_update_slice.70 = bf16[4,1024,256]{2,0,1:T(4,128)(2,1)} dynamic-update-slice(bf16[4,1024,256]{2,0,1:T(4,128)(2,1)} %get-tuple-element.1630, bf16[1,1024,256]{2,0,1:T(2,128)(2,1)} %copy.468, s32[]{:T(128)S(6)} %sub.482, s32[]{:T(128)} %constant.139.clone.1..sunk.1, s32[]{:T(128)} %constant.139.clone.1..sunk.1) | dynamic-update-slice | bytes 1048580 | tf_op jit(solution)/shard_map/transpose(jvp())/while/body/jit(dynamic_update_index_in_dim)/dynamic_update_slice | solution.py:89
  946.7 21.4 %dynamic_update_slice.70 = bf16[4,1024,256]{2,0,1:T(4,128)(2,1)} dynamic-update-slice(bf16[4,1024,256]{2,0,1:T(4,128)(2,1)} %get-tuple-element.1630, bf16[1,1024,256]{2,0,1:T(2,128)(2,1)} %copy.468, s32[]{:T(128)S(6)} %sub.482, s32[]{:T(128)} %constant.139.clone.1..sunk.1, s32[]{:T(128)} %constant.139.clone.1..sunk.1) | dynamic-update-slice | bytes 1048580 | tf_op jit(solution)/shard_map/transpose(jvp())/while/body/jit(dynamic_update_index_in_dim)/dynamic_update_slice | solution.py:89
  979.1 10.2 convolution_bitcast_fusion.11
  989.3 9.2 copy.265
  1016.5 67.3 %all-to-all-done.4 = bf16[4,1024,256]{2,0,1:T(4,128)(2,1)S(1)} async-done(((bf16[4,1024,256]{2,0,1:T(4,128)(2,1)}), bf16[4,1024,256]{2,0,1:T(4,128)(2,1)S(1)}, u32[]{:S(2)}, u32[]{:S(2)}) %all-to-all-start.4) | async-done | bytes 2097184 | tf_op jit(solution)/shard_map/all_to_all | solution.py:208
  1093.7 13.1 convolution_bitcast_fusion.10
  1132.7 11.4 fusion.186
  1144.1 39.6 %all-reduce.24 = (f32[1024]{0:T(1024)}, f32[4,2304]{1,0:T(4,128)}, f32[2304]{0:T(1024)}, f32[32]{0:T(128)}, f32[32]{0:T(128)}, /*index=5*/f32[32]{0:T(128)}, f32[2048]{0:T(1024)}) all-reduce(f32[1024]{0:T(1024)} %get-tuple-element.974, f32[4,2304]{1,0:T(4,128)} %pad_maximum_fusion.3, ...), channel_id=1, replica_groups=mesh['batch'=4,'seq'=8] {'batch','seq'}, use_global_device_ids=true, to_apply=%region_33.34 | all-reduce | flops 14688 | bytes 117504 | tf_op jit(solution)/shard_map/psum | solution.py:260
  1188.2 203.6 %reduce-scatter.8.cloned.1.call-done = f32[32,4384]{1,0:T(8,128)} async-done(((f32[1024,4384]{1,0:T(8,128)}), f32[32,4384]{1,0:T(8,128)}) %reduce-scatter.8.cloned.1.call-update) | async-done | bytes 561168 | tf_op jit(solution)/shard_map/reduce_scatter | solution.py:221
  (653 shorter events, 595.5 us)
Async XLA Ops:
  7.2 87.2 %all-gather.4.cloned.1.call-start = ((), (), s32[]{:S(2)}) async-start(), calls=%async_computation.9 | async-start | bytes 9461760 | tf_op jit(solution)/shard_map/all_gather | solution.py:126
  7.9 187.0 %all-gather.6.cloned.1.call-start = ((), (), s32[]{:S(2)}) async-start(), calls=%async_computation.10 | async-start | bytes 2359296 | tf_op jit(solution)/shard_map/all_gather | solution.py:142
  12.2 95.5 %copy-start.20 = (bf16[4,128,1024]{2,1,0:T(8,128)(2,1)}, bf16[4,128,1024]{2,1,0:T(8,128)(2,1)S(1)}, u32[]{:S(2)}) copy-start(bf16[4,128,1024]{2,1,0:T(8,128)(2,1)S(1)} %fusion.185) | copy-start | bytes 3145732
  111.9 9.1 all-to-all-start.1
  121.0 65.1 %all-to-all-start = ((bf16[4,128,2048]{1,0,2:T(4,128)(2,1)}), bf16[4,128,2048]{1,0,2:T(4,128)(2,1)S(1)}, u32[]{:S(2)}, u32[]{:S(2)}) async-start(bf16[4,128,2048]{1,0,2:T(4,128)(2,1)} %reshape.425), calls=%async_computation | async-start | bytes 4194304 | tf_op jit(solution)/shard_map/all_to_all | solution.py:139
  124.6 314.9 %all-gather.8.cloned.1.call-start = ((), (), s32[]{:S(2)}) async-start(), calls=%async_computation.11 | async-start | bytes 4325376 | tf_op jit(solution)/shard_map/all_gather | solution.py:173
  367.6 52.8 %all-to-all-start.2 = ((bf16[4,1024,256]{2,0,1:T(4,128)(2,1)}), bf16[4,1024,256]{2,0,1:T(4,128)(2,1)S(1)}, u32[]{:S(2)}, u32[]{:S(2)}) async-start(bf16[4,1024,256]{2,0,1:T(4,128)(2,1)} %get-tuple-element.719), calls=%async_computation.2 | async-start | bytes 4194304 | tf_op jit(solution)/shard_map/all_to_all | solution.py:166
  456.6 52.6 %all-to-all-start.3 = ((bf16[4,128,2048]{1,0,2:T(4,128)(2,1)}), bf16[4,128,2048]{1,0,2:T(4,128)(2,1)S(1)}, u32[]{:S(2)}, u32[]{:S(2)}) async-start(bf16[4,128,2048]{1,0,2:T(4,128)(2,1)} %copy.234), calls=%async_computation.3 | async-start | bytes 4194304 | tf_op jit(solution)/shard_map/all_to_all | solution.py:194
  460.3 633.5 %reduce-scatter.6.cloned.1.call-start = ((), (), s32[]{:S(2)}) async-start(), calls=%async_computation.12 | async-start | bytes 2359296 | tf_op jit(solution)/shard_map/reduce_scatter | solution.py:213
  522.2 456.9 %copy-start.27 = (f32[2048]{0:T(1024)S(1)}, f32[2048]{0:T(1024)}, u32[]{:S(2)}) copy-start(f32[2048]{0:T(1024)} %param.24) | copy-start | bytes 24580
  522.2 457.0 %copy-start.35 = (f32[4,128]{1,0:T(4,128)S(1)}, f32[4,128]{1,0:T(4,128)}, u32[]{:S(2)}) copy-start(f32[4,128]{1,0:T(4,128)} %copy-done.34) | copy-start | bytes 6148
  600.9 29.0 %copy-start.8 = (f32[1024,256]{0,1:T(8,128)S(1)}, f32[1024,256]{0,1:T(8,128)}, u32[]{:S(2)}) copy-start(f32[1024,256]{0,1:T(8,128)} %get-tuple-element.1529) | copy-start | bytes 3145732 | tf_op jit(solution)/shard_map/transpose(jvp())/while
  600.9 29.0 %copy-start.9 = (f32[1024,256]{0,1:T(8,128)S(1)}, f32[1024,256]{0,1:T(8,128)}, u32[]{:S(2)}) copy-start(f32[1024,256]{0,1:T(8,128)} %get-tuple-element.1528) | copy-start | bytes 3145732 | tf_op jit(solution)/shard_map/transpose(jvp())/while
  600.9 29.0 %copy-start.10 = (f32[1024,256]{0,1:T(8,128)S(1)}, f32[1024,256]{0,1:T(8,128)}, u32[]{:S(2)}) copy-start(f32[1024,256]{0,1:T(8,128)} %get-tuple-element.1527) | copy-start | bytes 3145732 | tf_op jit(solution)/shard_map/transpose(jvp())/while
  713.7 29.0 %copy-start.8 = (f32[1024,256]{0,1:T(8,128)S(1)}, f32[1024,256]{0,1:T(8,128)}, u32[]{:S(2)}) copy-start(f32[1024,256]{0,1:T(8,128)} %get-tuple-element.1529) | copy-start | bytes 3145732 | tf_op jit(solution)/shard_map/transpose(jvp())/while
  713.7 29.0 %copy-start.9 = (f32[1024,256]{0,1:T(8,128)S(1)}, f32[1024,256]{0,1:T(8,128)}, u32[]{:S(2)}) copy-start(f32[1024,256]{0,1:T(8,128)} %get-tuple-element.1528) | copy-start | bytes 3145732 | tf_op jit(solution)/shard_map/transpose(jvp())/while
  826.4 29.0 %copy-start.8 = (f32[1024,256]{0,1:T(8,128)S(1)}, f32[1024,256]{0,1:T(8,128)}, u32[]{:S(2)}) copy-start(f32[1024,256]{0,1:T(8,128)} %get-tuple-element.1529) | copy-start | bytes 3145732 | tf_op jit(solution)/shard_map/transpose(jvp())/while
  826.4 29.0 %copy-start.9 = (f32[1024,256]{0,1:T(8,128)S(1)}, f32[1024,256]{0,1:T(8,128)}, u32[]{:S(2)}) copy-start(f32[1024,256]{0,1:T(8,128)} %get-tuple-element.1528) | copy-start | bytes 3145732 | tf_op jit(solution)/shard_map/transpose(jvp())/while
  939.1 29.0 %copy-start.8 = (f32[1024,256]{0,1:T(8,128)S(1)}, f32[1024,256]{0,1:T(8,128)}, u32[]{:S(2)}) copy-start(f32[1024,256]{0,1:T(8,128)} %get-tuple-element.1529) | copy-start | bytes 3145732 | tf_op jit(solution)/shard_map/transpose(jvp())/while
  939.1 29.0 %copy-start.9 = (f32[1024,256]{0,1:T(8,128)S(1)}, f32[1024,256]{0,1:T(8,128)}, u32[]{:S(2)}) copy-start(f32[1024,256]{0,1:T(8,128)} %get-tuple-element.1528) | copy-start | bytes 3145732 | tf_op jit(solution)/shard_map/transpose(jvp())/while
  979.1 209.2 %reduce-scatter.10.cloned.1.call-start = ((), (), s32[]{:S(2)}) async-start(), calls=%async_computation.14 | async-start | bytes 8650752
  1009.6 74.2 %all-to-all-start.4 = ((bf16[4,1024,256]{2,0,1:T(4,128)(2,1)}), bf16[4,1024,256]{2,0,1:T(4,128)(2,1)S(1)}, u32[]{:S(2)}, u32[]{:S(2)}) async-start(bf16[4,1024,256]{2,0,1:T(4,128)(2,1)} %get-tuple-element.720), calls=%async_computation.4 | async-start | bytes 4194304 | tf_op jit(solution)/shard_map/all_to_all | solution.py:208
  1013.3 378.5 %reduce-scatter.8.cloned.1.call-start = ((), (), s32[]{:S(2)}) async-start(), calls=%async_computation.13 | async-start | bytes 18923520 | tf_op jit(solution)/shard_map/reduce_scatter | solution.py:221
  1132.7 51.7 %copy-start.29 = (f32[4,128]{1,0:T(4,128)S(1)}, f32[4,128]{1,0:T(4,128)}, u32[]{:S(2)}) copy-start(f32[4,128]{1,0:T(4,128)} %copy-done.28) | copy-start | bytes 6148
  (72 other events, 405.1 us)
Sparse Core Ops, SparseCore 0:
  10.9 83.4 all-gather.3
  110.6 42.7 all-gather.5
  156.4 70.9 all-gather.7
  979.2 34.5 reduce-scatter.5
  1016.5 170.8 reduce-scatter.9
  1190.1 201.6 reduce-scatter.7
where the time goes:
time: 1430 us; the launch traced here: 1400 us
  waiting for transfers between devices  497 us (35%)
  local copies, waits for them, and re-layouts  395 us (28%)
  matrix products  274 us (19%)
  other arithmetic  143 us (10%)
  blocking collectives  48 us (3%)
  starting transfers between devices  18.2 us (1%)
  between operations  14.8 us (1%)
    reduce_scatter x1, waiting for transfers between devices, local(): lax.psum_scatter(lax.dot_general(part, proj_grad, contract_first, preferr...  204 us
    dynamic_update_slice x28, local copies, waits for them, and re-layouts, mixer_block(): return lax.map(jax.checkpoint(single_row), (x_heads, step_heads, bc_all))  199 us
    dot_general x12, matrix products, state_space(): y_diag = jnp.einsum('chij,cjhp->cihp', weights, x_blocks, precision=HIGH)  83 us
    all_gather x1, waiting for transfers between devices, local(): lax.all_gather(inproj_weight, ('batch', 'seq'), axis=0, tiled=True)  82.2 us
    all_to_all x1, waiting for transfers between devices, local(): lax.all_to_all(x_grad.astype(jnp.bfloat16), 'seq', split_axis=1, concat_a...  67.3 us
    all_to_all x1, waiting for transfers between devices, local(): lax.all_to_all(x_send, 'seq', split_axis=2, concat_axis=1, tiled=True)  58.7 us
    all_to_all x1, waiting for transfers between devices, local(): lax.all_to_all(y_grad_low, 'seq', split_axis=2, concat_axis=1, tiled=True)  48 us
    mul x16, other arithmetic, causal_filter(): total = total + taps[offset][None, :] * padded[offset:offset + length]  43.7 us
  transfers between devices with their start and end apart: 11, of which 7 were waited for; matrix products, arithmetic and copies ran while one was open for 22% of the time, Pallas kernels for 0%

commit v1 on v0

v1 whole, which is shorter than its diff:
```python
import functools

import jax
import jax.numpy as jnp
from jax import lax
from jax.experimental import pallas as pl
from jax.experimental.pallas import tpu as pltpu
from jax.sharding import PartitionSpec as P

HEADS = 32
HEADDIM = 64
STATE = 128
CONV = 4
INNER = 2048
PROJ = 4384
EPS = 1e-05
HIGH = lax.Precision.HIGHEST
HALO = CONV - 1
PIECE = 32


def chain_kernel(forward, local_ref, dec_ref, out_ref, sent, held, send_sem, recv_sem):
    size = lax.axis_size("seq")
    me = lax.axis_index("seq")
    up = lax.rem(me + 1, size)
    down = lax.rem(me + size - 1, size)
    target = up if forward else down
    gets = me > 0 if forward else me < size - 1
    gives = me < size - 1 if forward else me > 0
    barrier = pltpu.get_barrier_semaphore()
    for other in (up, down):
        pl.semaphore_signal(
            barrier, inc=1, device_id={"seq": other}, device_id_type=pl.DeviceIdType.MESH
        )
    pl.semaphore_wait(barrier, 2)
    seqs, states, _ = local_ref.shape
    per = states // PIECE

    def copy_of(p):
        return pltpu.make_async_remote_copy(
            src_ref=sent.at[p],
            dst_ref=held.at[p],
            send_sem=send_sem.at[p],
            recv_sem=recv_sem.at[p],
            device_id={"seq": target},
            device_id_type=pl.DeviceIdType.MESH,
        )

    def step(p, carry):
        q = p // per
        rows = pl.ds(pl.multiple_of((p % per) * PIECE, PIECE), PIECE)

        @pl.when(gets)
        def _():
            copy_of(p).wait_recv()
            out_ref[q, rows, :] = held[p]

        @pl.when(jnp.logical_not(gets))
        def _():
            out_ref[q, rows, :] = jnp.zeros((PIECE, out_ref.shape[2]), out_ref.dtype)

        @pl.when(gives)
        def _():
            value = out_ref[q, rows, :].astype(jnp.float32) * dec_ref[q] + local_ref[q, rows, :]
            sent[p] = value.astype(sent.dtype)
            copy_of(p).start()

        return carry

    lax.fori_loop(0, seqs * per, step, 0)

    @pl.when(gives)
    def _():
        def finish(p, carry):
            copy_of(p).wait_send()
            return carry

        lax.fori_loop(0, seqs * per, finish, 0)


def run_chain(local_state, dec, forward):
    seqs, states, width = local_state.shape
    pieces = seqs * (states // PIECE)
    return pl.pallas_call(
        functools.partial(chain_kernel, forward),
        out_shape=jax.ShapeDtypeStruct(local_state.shape, jnp.bfloat16),
        in_specs=[pl.BlockSpec(memory_space=pltpu.VMEM)] * 2,
        out_specs=pl.BlockSpec(memory_space=pltpu.VMEM),
        scratch_shapes=[
            pltpu.VMEM((pieces, PIECE, width), jnp.bfloat16),
            pltpu.VMEM((pieces, PIECE, width), jnp.bfloat16),
            pltpu.SemaphoreType.DMA((pieces,)),
            pltpu.SemaphoreType.DMA((pieces,)),
        ],
        compiler_params=pltpu.CompilerParams(
            collective_id=0 if forward else 1,
            has_side_effects=True,
            vmem_limit_bytes=40 * 1024 * 1024,
        ),
        name="chain_up" if forward else "chain_down",
    )(local_state, dec)


GROUP = 8
WIDE = GROUP * HEADDIM
PAIRS = GROUP // 2
BF = jnp.bfloat16
F32 = jnp.float32
LAST = (((1,), (1,)), ((), ()))
FIRST = (((0,), (0,)), ((), ()))
MIB = 1024 * 1024


def mul(a, b, dims=(((1,), (0,)), ((), ()))):
    return lax.dot_general(a, b, dims, preferred_element_type=F32)


def left_half(rows):
    return lax.broadcasted_iota(jnp.int32, (rows, 128), 1) < HEADDIM


def spread(cols, pair, sel):
    return jnp.where(sel, cols[:, 2 * pair : 2 * pair + 1], cols[:, 2 * pair + 1 : 2 * pair + 2])


def halves(v, sel):
    zero = jnp.zeros_like(v)
    return jnp.concatenate([jnp.where(sel, v, zero), jnp.where(sel, zero, v)], 0)


def conv_pre(x_ref, halo_ref, taps_ref, bias_ref, ext):
    length = x_ref.shape[0]
    ext[0:8, :] = halo_ref[0].astype(F32)
    ext[8 : 8 + length, :] = x_ref[...].astype(BF).astype(F32)
    pre = bias_ref[...]
    for k in range(CONV):
        pre = pre + taps_ref[k : k + 1, :] * ext[5 + k : 5 + k + length, :]
    return pre


def decays(cum, cum_t, head, lower):
    gap = cum[:, head : head + 1] - cum_t[head : head + 1, :]
    return jnp.where(lower, jnp.exp(gap), 0.0)


def lower_mask(length):
    return lax.broadcasted_iota(jnp.int32, (length, length), 0) >= lax.broadcasted_iota(
        jnp.int32, (length, length), 1
    )


def forward_kernel(
    x_ref, halo_ref, taps_ref, bias_ref, b_ref, c_ref, step_ref, cum_ref, cumt_ref, skip_ref,
    y_ref, state_ref, dec_ref, ext,
):
    pre = conv_pre(x_ref, halo_ref, taps_ref, bias_ref, ext)
    x = pre * jax.nn.sigmoid(pre)
    length = x.shape[0]
    b, c = b_ref[0].astype(BF), c_ref[0].astype(BF)
    scores = mul(c, b, LAST)
    lower = lower_mask(length)
    sel = left_half(length)
    step, cum, cum_t = step_ref[0, 0], cum_ref[0, 0], cumt_ref[0, 0]
    for j in range(PAIRS):
        cols = slice(128 * j, 128 * j + 128)
        xp = x[:, cols]
        xd = xp * spread(step, j, sel)
        cumx = spread(cum, j, sel)
        last = cumx[length - 1 : length, :]
        w = jnp.concatenate(
            [(scores * decays(cum, cum_t, 2 * j + i, lower)).astype(BF) for i in range(2)], 1
        )
        y_ref[0, :, cols] = mul(w, halves(xd.astype(BF), sel)) + skip_ref[:, cols] * xp
        state_ref[0, :, cols] = mul(b, (jnp.exp(last - cumx) * xd).astype(BF), FIRST)
        dec_ref[0, :, cols] = jnp.exp(last)


def finish_kernel(y_ref, start_ref, c_ref, cum_ref, gate_ref, gain_ref, sent_ref, norm_ref):
    length = y_ref.shape[1]
    sel = left_half(length)
    c = c_ref[0].astype(BF)
    squares = jnp.zeros((length, 1), F32)
    for j in range(HEADS // 2):
        cols = slice(128 * j, 128 * j + 128)
        cumx = spread(cum_ref[0], j, sel)
        y = y_ref[0, :, cols] + jnp.exp(cumx) * mul(c, start_ref[0, :, cols])
        y = y.astype(BF)
        sent_ref[:, cols] = y
        gate = gate_ref[:, cols]
        gated = y.astype(F32) * (gate * jax.nn.sigmoid(gate))
        squares = squares + jnp.sum(gated * gated, 1, keepdims=True)
    q = lax.rsqrt(squares / INNER + EPS)
    for j in range(HEADS // 2):
        cols = slice(128 * j, 128 * j + 128)
        gate = gate_ref[:, cols]
        gated = sent_ref[:, cols].astype(F32) * (gate * jax.nn.sigmoid(gate))
        norm_ref[:, cols] = (gated * q * gain_ref[:, cols]).astype(BF)


def post_kernel(
    grad_ref, sent_ref, gate_ref, gain_ref, c_ref, cum_ref,
    gate_grad_ref, y_grad_ref, gain_grad_ref, state_grad_ref,
):
    length = grad_ref.shape[0]
    sel = left_half(length)
    c = c_ref[0].astype(BF)
    squares = jnp.zeros((length, 1), F32)
    dots = jnp.zeros((length, 1), F32)
    for j in range(HEADS // 2):
        cols = slice(128 * j, 128 * j + 128)
        gate = gate_ref[:, cols]
        gated = sent_ref[:, cols].astype(F32) * (gate * jax.nn.sigmoid(gate))
        squares = squares + jnp.sum(gated * gated, 1, keepdims=True)
        dots = dots + jnp.sum(gated * grad_ref[:, cols] * gain_ref[:, cols], 1, keepdims=True)
    q = lax.rsqrt(squares / INNER + EPS)
    back = q * q * q * (dots / INNER)

    @pl.when(pl.program_id(0) == 0)
    def _():
        gain_grad_ref[...] = jnp.zeros_like(gain_grad_ref)

    for j in range(HEADS // 2):
        cols = slice(128 * j, 128 * j + 128)
        gate = gate_ref[:, cols]
        sg = jax.nn.sigmoid(gate)
        act = gate * sg
        y = sent_ref[:, cols].astype(F32)
        gated = y * act
        grad = grad_ref[:, cols]
        gain_grad_ref[:, cols] += jnp.sum(grad * gated * q, 0, keepdims=True)
        inner = q * (grad * gain_ref[:, cols]) - gated * back
        gate_grad_ref[:, cols] = (inner * y * (sg * (1.0 + gate * (1.0 - sg)))).astype(BF)
        dy = (inner * act).astype(BF)
        y_grad_ref[:, cols] = dy
        cumx = spread(cum_ref[0], j, sel)
        state_grad_ref[0, :, cols] = mul(
            c, (jnp.exp(cumx) * dy.astype(F32)).astype(BF), FIRST
        )


def backward_kernel(
    x_ref, halo_ref, taps_ref, bias_ref, b_ref, c_ref, step_ref, cum_ref, cumt_ref, skip_ref,
    dy_ref, right_ref, start_ref,
    back_ref, head_ref, stats_ref, dstep_ref, dcum_ref, dcumt_ref, db_ref, dc_ref, ext, late,
):
    pre = conv_pre(x_ref, halo_ref, taps_ref, bias_ref, ext)
    length = pre.shape[0]
    b, c = b_ref[0].astype(BF), c_ref[0].astype(BF)
    scores = mul(c, b, LAST)
    lower = lower_mask(length)
    sel = left_half(length)
    step, cum, cum_t = step_ref[0, 0], cum_ref[0, 0], cumt_ref[0, 0]
    d_scores = jnp.zeros((length, length), F32)
    db = jnp.zeros((length, STATE), F32)
    dc = jnp.zeros((length, STATE), F32)
    late[length : length + 8, :] = jnp.zeros((8, WIDE), F32)
    for j in range(PAIRS):
        cols = slice(128 * j, 128 * j + 128)
        prep = pre[:, cols]
        sg = jax.nn.sigmoid(prep)
        xp = prep * sg
        stx = spread(step, j, sel)
        xd = xp * stx
        cumx = spread(cum, j, sel)
        last = cumx[length - 1 : length, :]
        dy_low = dy_ref[:, cols]
        dy = dy_low.astype(F32)
        dy_halves = halves(dy_low, sel)
        m = mul(dy_halves, xd.astype(BF), LAST)
        weights, row_sums = [], []
        for i in range(2):
            h = 2 * j + i
            e = decays(cum, cum_t, h, lower)
            weights.append((scores * e).astype(BF))
            me = m[i * length : (i + 1) * length] * e
            d_scores = d_scores + me
            mge = me * scores
            row_sums.append(jnp.sum(mge, 1, keepdims=True))
            dcumt_ref[0, 0, h : h + 1, :] = jnp.sum(mge, 0, keepdims=True)
        ends = jnp.exp(last - cumx)
        starts = jnp.exp(cumx)
        right, start = right_ref[0, :, cols], start_ref[0, :, cols]
        b_right = ends * mul(b, right)
        dxd = mul(jnp.concatenate(weights, 0), dy_halves, FIRST) + b_right
        dy_start = starts * dy
        xd_end = b_right * xd
        moved = dy_start * mul(c, start) - xd_end
        d_st = dxd * xp
        zero = jnp.zeros_like(moved)
        for i in range(2):
            h = 2 * j + i
            keep = sel if i == 0 else jnp.logical_not(sel)
            dcum_ref[0, 0, :, h : h + 1] = row_sums[i] + jnp.sum(
                jnp.where(keep, moved, zero), 1, keepdims=True
            )
            dstep_ref[0, 0, :, h : h + 1] = jnp.sum(jnp.where(keep, d_st, zero), 1, keepdims=True)
        d_last = jnp.sum(xd_end, 0, keepdims=True) + jnp.exp(last) * jnp.sum(
            right.astype(F32) * start.astype(F32), 0, keepdims=True
        )
        dx = stx * dxd + skip_ref[:, cols] * dy
        pre_grad = dx * (sg * (1.0 + prep * (1.0 - sg)))
        late[0:length, cols] = pre_grad
        stats_ref[0, CONV : CONV + 1, cols] = jnp.sum(pre_grad, 0, keepdims=True)
        stats_ref[0, CONV + 1 : CONV + 2, cols] = jnp.sum(xp * dy, 0, keepdims=True)
        stats_ref[0, CONV + 2 : CONV + 3, cols] = d_last
        for k in range(CONV):
            stats_ref[0, k : k + 1, cols] = jnp.sum(
                pre_grad * ext[5 + k : 5 + k + length, cols], 0, keepdims=True
            )
        db = db + mul((ends * xd).astype(BF), right, LAST)
        dc = dc + mul(dy_start.astype(BF), start, LAST)
    stats_ref[0, CONV + 3 : CONV + 4, :] = jnp.zeros((1, WIDE), F32)
    low = d_scores.astype(BF)
    db = db + mul(low, c, FIRST)
    dc = dc + mul(low, b)
    first = pl.program_id(1) == 0

    @pl.when(first)
    def _():
        db_ref[0] = db
        dc_ref[0] = dc

    @pl.when(jnp.logical_not(first))
    def _():
        db_ref[0] += db
        dc_ref[0] += dc

    total = taps_ref[0:1, :] * late[HALO : HALO + length, :]
    for k in range(1, CONV):
        total = total + taps_ref[k : k + 1, :] * late[HALO - k : HALO - k + length, :]
    back_ref[...] = total
    head_ref[0] = late[0:8, :]


def causal_filter(values, taps, bias):
    length = values.shape[1] - HALO
    total = bias[None, None, :]
    for offset in range(CONV):
        total = total + taps[offset][None, None, :] * values[:, offset : offset + length]
    return total


def bc_part(values, taps, bias):
    return jax.nn.silu(causal_filter(values, taps, bias))


def step_part(sent, bias, decay_log):
    step = jax.nn.softplus(sent + bias[None, None, :])
    a = step * (-jnp.exp(decay_log))[None, None, :]
    lower = lower_mask(sent.shape[1]).astype(F32)
    return step, jnp.einsum("ij,qjh->qih", lower, a, precision=HIGH)


def params(semantics):
    return pltpu.CompilerParams(
        dimension_semantics=semantics, vmem_limit_bytes=40 * MIB
    )


def prenorm(row, gain):
    return row * lax.rsqrt(jnp.mean(row * row, -1, keepdims=True) + EPS) * gain


def local(
    tokens,
    cotangent,
    prenorm_gain,
    inproj_weight,
    conv_taps,
    conv_bias,
    step_bias,
    decay_log,
    skip_weight,
    postnorm_gain,
    outproj_weight,
):
    seqs, length, width = tokens.shape
    rows = seqs * length
    groups = HEADS // GROUP
    size = lax.axis_size("seq")
    up = [(i, i + 1) for i in range(size - 1)]
    down = [(i + 1, i) for i in range(size - 1)]
    both = ("batch", "seq")
    inproj_full = lax.all_gather(inproj_weight, both, axis=0, tiled=True)
    outproj_full = lax.all_gather(outproj_weight, both, axis=0, tiled=True)
    token_f = tokens.astype(F32)
    normed_f, pre_back = jax.vjp(prenorm, token_f, prenorm_gain)
    normed = normed_f.astype(BF).reshape(rows, width)
    proj = jnp.dot(normed, inproj_full, preferred_element_type=F32)
    by_seq = proj.reshape(seqs, length, PROJ)
    halo = lax.ppermute(
        by_seq[:, length - HALO :, INNER : 2 * INNER + 2 * STATE].astype(BF), "seq", up
    )
    halo_x = jnp.pad(halo[..., :INNER], ((0, 0), (8 - HALO, 0), (0, 0)))
    bc_sent = by_seq[..., 2 * INNER : 2 * INNER + 2 * STATE].astype(BF)
    bc_ext = jnp.concatenate([halo[..., INNER:], bc_sent], 1).astype(F32)
    bc_conv, bc_vjp = jax.vjp(bc_part, bc_ext, conv_taps[:, INNER:], conv_bias[INNER:])
    step_sent = by_seq[..., 2 * INNER + 2 * STATE :].astype(BF).astype(F32)
    (step, cum), step_vjp = jax.vjp(step_part, step_sent, step_bias, decay_log)

    def grouped(v):
        return v.reshape(seqs, length, groups, GROUP).transpose(0, 2, 1, 3)

    def ungrouped(v):
        return v.transpose(0, 2, 1, 3).reshape(seqs, length, HEADS)

    step_g, cum_g = grouped(step), grouped(cum)
    cum_t = cum.transpose(0, 2, 1).reshape(seqs, groups, GROUP, length)
    skip = jnp.repeat(skip_weight, HEADDIM)[None, :]
    bias = conv_bias[None, :]
    gain = postnorm_gain[None, :]
    offset = INNER // WIDE
    mixer_specs = [
        pl.BlockSpec((length, WIDE), lambda q, g: (q, offset + g)),
        pl.BlockSpec((1, 8, WIDE), lambda q, g: (q, 0, g)),
        pl.BlockSpec((CONV, WIDE), lambda q, g: (0, g)),
        pl.BlockSpec((1, WIDE), lambda q, g: (0, g)),
        pl.BlockSpec((1, length, STATE), lambda q, g: (q, 0, 0)),
        pl.BlockSpec((1, length, STATE), lambda q, g: (q, 0, 1)),
        pl.BlockSpec((1, 1, length, GROUP), lambda q, g: (q, g, 0, 0)),
        pl.BlockSpec((1, 1, length, GROUP), lambda q, g: (q, g, 0, 0)),
        pl.BlockSpec((1, 1, GROUP, length), lambda q, g: (q, g, 0, 0)),
        pl.BlockSpec((1, WIDE), lambda q, g: (0, g)),
    ]
    mixer_args = (
        proj, halo_x, conv_taps, bias, bc_conv, bc_conv, step_g, cum_g, cum_t, skip,
    )
    row_block = pl.BlockSpec((length, WIDE), lambda q, g: (q, g))
    state_block = pl.BlockSpec((1, STATE, WIDE), lambda q, g: (q, 0, g))

    def shape(dims, kind=F32):
        return jax.ShapeDtypeStruct(dims, kind)

    y_local, state, dec = pl.pallas_call(
        forward_kernel,
        grid=(seqs, groups),
        in_specs=mixer_specs,
        out_specs=[
            pl.BlockSpec((1, length, WIDE), lambda q, g: (q, 0, g)),
            state_block,
            pl.BlockSpec((1, 1, WIDE), lambda q, g: (q, 0, g)),
        ],
        out_shape=[
            shape((seqs, length, INNER)),
            shape((seqs, STATE, INNER)),
            shape((seqs, 1, INNER)),
        ],
        scratch_shapes=[pltpu.VMEM((length + 8, WIDE), F32)],
        compiler_params=params(("arbitrary", "arbitrary")),
        name="mixer_forward",
    )(*mixer_args)
    start = run_chain(state, dec, True)
    full_rows = pl.BlockSpec((length, INNER), lambda q: (q, 0))
    full_seq = pl.BlockSpec((1, length, INNER), lambda q: (q, 0, 0))
    full_gain = pl.BlockSpec((1, INNER), lambda q: (0, 0))
    c_block = pl.BlockSpec((1, length, STATE), lambda q: (q, 0, 1))
    cum_block = pl.BlockSpec((1, length, HEADS), lambda q: (q, 0, 0))
    y_sent, y_norm = pl.pallas_call(
        finish_kernel,
        grid=(seqs,),
        in_specs=[full_seq, full_seq, c_block, cum_block, full_rows, full_gain],
        out_specs=[full_rows, full_rows],
        out_shape=[shape((rows, INNER), BF), shape((rows, INNER), BF)],
        compiler_params=params(("arbitrary",)),
        name="mixer_finish",
    )(y_local, start, bc_conv, cum, proj, gain)
    branch = mul(y_norm, outproj_full, LAST)
    mixed = (token_f + branch.reshape(seqs, length, width)).astype(BF)
    upstream = cotangent.reshape(rows, width)
    outproj_grad = lax.psum_scatter(
        mul(upstream, y_norm, FIRST).astype(BF), both, scatter_dimension=0, tiled=True
    ).astype(F32)
    norm_grad = mul(upstream, outproj_full)
    gate_grad, y_grad, gain_grad, state_grad = pl.pallas_call(
        post_kernel,
        grid=(seqs,),
        in_specs=[full_rows, full_rows, full_rows, full_gain, c_block, cum_block],
        out_specs=[full_rows, full_rows, full_gain, full_seq],
        out_shape=[
            shape((rows, INNER), BF),
            shape((rows, INNER), BF),
            shape((1, INNER)),
            shape((seqs, STATE, INNER)),
        ],
        compiler_params=params(("arbitrary",)),
        name="post_backward",
    )(norm_grad, y_sent, proj, gain, bc_conv, cum)
    right = run_chain(state_grad, dec, False)
    back, head, stats, dstep, dcum, dcum_t, db, dc = pl.pallas_call(
        backward_kernel,
        grid=(seqs, groups),
        in_specs=mixer_specs + [row_block, state_block, state_block],
        out_specs=[
            row_block,
            pl.BlockSpec((1, 8, WIDE), lambda q, g: (q, 0, g)),
            pl.BlockSpec((1, 8, WIDE), lambda q, g: (q, 0, g)),
            pl.BlockSpec((1, 1, length, GROUP), lambda q, g: (q, g, 0, 0)),
            pl.BlockSpec((1, 1, length, GROUP), lambda q, g: (q, g, 0, 0)),
            pl.BlockSpec((1, 1, GROUP, length), lambda q, g: (q, g, 0, 0)),
            pl.BlockSpec((1, length, STATE), lambda q, g: (q, 0, 0)),
            pl.BlockSpec((1, length, STATE), lambda q, g: (q, 0, 0)),
        ],
        out_shape=[
            shape((rows, INNER)),
            shape((seqs, 8, INNER)),
            shape((seqs, 8, INNER)),
            shape((seqs, groups, length, GROUP)),
            shape((seqs, groups, length, GROUP)),
            shape((seqs, groups, GROUP, length)),
            shape((seqs, length, STATE)),
            shape((seqs, length, STATE)),
        ],
        scratch_shapes=[
            pltpu.VMEM((length + 8, WIDE), F32),
            pltpu.VMEM((length + 8, WIDE), F32),
        ],
        compiler_params=params(("arbitrary", "arbitrary")),
        name="mixer_backward",
    )(*mixer_args, y_grad, right, start)
    d_last = stats[:, CONV + 2].reshape(seqs, HEADS, HEADDIM).sum(-1)
    cum_grad = ungrouped(dcum) - dcum_t.reshape(seqs, HEADS, length).transpose(0, 2, 1)
    at_last = (jnp.arange(length) == length - 1)[None, :, None]
    cum_grad = cum_grad + jnp.where(at_last, d_last[:, None, :], 0.0)
    step_back, step_full, decay_full = step_vjp((ungrouped(dstep), cum_grad))
    bc_grad, taps_bc_grad, bias_bc_grad = bc_vjp(jnp.concatenate([db, dc], 2))
    per_channel = stats.sum(0)
    skip_full = per_channel[CONV + 1].reshape(HEADS, HEADDIM).sum(-1)
    taps_full = jnp.concatenate([per_channel[:CONV], taps_bc_grad], 1)
    bias_full = jnp.concatenate([per_channel[CONV], bias_bc_grad])
    head_x = jnp.stack(
        [
            sum(
                conv_taps[k, :INNER] * head[:, i + HALO - k - HALO]
                for k in range(CONV)
                if 0 <= i - k < HALO
            )
            for i in range(HALO)
        ],
        1,
    )
    tail = lax.ppermute(jnp.concatenate([head_x, bc_grad[:, :HALO]], 2), "seq", down)
    x_back = back.reshape(seqs, length, INNER)
    keep = length - HALO
    proj_grad = jnp.concatenate(
        [
            gate_grad.reshape(seqs, length, INNER),
            jnp.concatenate(
                [x_back[:, :keep], x_back[:, keep:] + tail[..., :INNER]], 1
            ).astype(BF),
            jnp.concatenate(
                [bc_grad[:, HALO:length], bc_grad[:, length:] + tail[..., INNER:]], 1
            ).astype(BF),
            step_back.astype(BF),
        ],
        2,
    ).reshape(rows, PROJ)
    inproj_grad = lax.psum_scatter(
        mul(normed, proj_grad, FIRST).astype(BF), both, scatter_dimension=0, tiled=True
    ).astype(F32)
    normed_grad = mul(proj_grad, inproj_full, LAST)
    token_grad, prenorm_part = pre_back(normed_grad.reshape(seqs, length, width))
    input_grad = cotangent.astype(F32) + token_grad
    summed = lax.psum(
        (prenorm_part, taps_full, bias_full, step_full, decay_full, skip_full, gain_grad[0]),
        both,
    )
    return (
        mixed,
        input_grad,
        summed[0],
        inproj_grad,
        summed[1],
        summed[2],
        summed[3],
        summed[4],
        summed[5],
        summed[6],
        outproj_grad,
    )


def solution(mesh):
    in_specs = (
        P("batch", "seq", None),
        P("batch", "seq", None),
        P(),
        P(("batch", "seq"), None),
        P(),
        P(),
        P(),
        P(),
        P(),
        P(),
        P(("batch", "seq"), None),
    )
    out_specs = (
        P("batch", "seq", None),
        P("batch", "seq", None),
        P(),
        P(("batch", "seq"), None),
        P(),
        P(),
        P(),
        P(),
        P(),
        P(),
        P(("batch", "seq"), None),
    )
    return jax.shard_map(local, mesh=mesh, in_specs=in_specs, out_specs=out_specs, check_vma=False)
```

time: 1430 us -> 519 us (0.36); the launches traced: 1400 us -> 517 us
  local copies, waits for them, and re-layouts: 395 us -> 45.5 us
  waiting for transfers between devices: 497 us -> 174 us
  matrix products: 274 us -> 56.4 us
  Pallas kernels: 0 us -> 161 us
  other arithmetic: 143 us -> 19.5 us
  starting transfers between devices: 18.2 us -> 3.82 us
    all_to_all x5 -> x0, waiting for transfers between devices: 210 us -> none  [the longest x1 67.3 us: local(): lax.all_to_all(x_grad.astype(jnp.bfloat16), 'seq', split_axis=1, concat_a...]
    dot_general x98 -> x8, matrix products: 266 us -> 56.4 us  [the longest x5 38.7 us: mul(): return lax.dot_general(a, b, dims, preferred_element_type=F32)]
    dynamic_update_slice x33 -> x0, local copies, waits for them, and re-layouts: 204 us -> none  [the longest x28 199 us: mixer_block(): return lax.map(jax.checkpoint(single_row), (x_heads, step_heads, bc_all))]
    pallas_call x0 -> x6, Pallas kernels: none -> 161 us  [the longest x2 91.8 us: run_chain(): pl.pallas_call(functools.partial(chain_kernel, forward), out_shape=jax.Sh...]
    reduce_scatter x2 -> x1, waiting for transfers between devices: 204 us -> 92.9 us  [local(): lax.psum_scatter(mul(normed, proj_grad, FIRST).astype(BF), both, scatter_...]
    mul x44 -> x3, other arithmetic: 69.7 us -> 2.6 us  [the longest x1 1.16 us: bc_part(): return jax.nn.silu(causal_filter(values, taps, bias))]
    convert_element_type x15 -> x0, local copies, waits for them, and re-layouts: 44.2 us -> none  [the longest x3 13.3 us: local(): y_tokens.astype(jnp.float32)]
    reshape x29 -> x5, local copies, waits for them, and re-layouts: 47.1 us -> 3.19 us  [the longest x2 1.68 us: ungrouped(): return v.transpose(0, 2, 1, 3).reshape(seqs, length, HEADS)]
  transfers between devices with their start and end apart: 11 -> 6, of which waited for: 7 -> 2; matrix products, arithmetic and copies ran while one was open for 22% -> 22% of each run, Pallas kernels for 0% -> 31%
where the time goes in v1:
time: 519 us; the launch traced here: 517 us
  waiting for transfers between devices  174 us (34%)
  Pallas kernels  161 us (31%)
  matrix products  56.4 us (11%)
  local copies, waits for them, and re-layouts  45.5 us (9%)
  blocking collectives  42.3 us (8%)
  other arithmetic  19.5 us (4%)
  between operations  14.5 us (3%)
    reduce_scatter x1, waiting for transfers between devices, local(): lax.psum_scatter(mul(normed, proj_grad, FIRST).astype(BF), both, scatter_...  92.9 us
    pallas_call x2, Pallas kernels, run_chain(): pl.pallas_call(functools.partial(chain_kernel, forward), out_shape=jax.Sh...  91.8 us
    all_gather x1, waiting for transfers between devices, local(): inproj_full = lax.all_gather(inproj_weight, both, axis=0, tiled=True)  79.6 us
    psum x1, blocking collectives, local(): lax.psum((prenorm_part, taps_full, bias_full, step_full, decay_full, skip...  42.3 us
    dot_general x5, matrix products, mul(): return lax.dot_general(a, b, dims, preferred_element_type=F32)  38.7 us
    pallas_call x1, Pallas kernels, local(): pl.pallas_call(backward_kernel, grid=(seqs, groups), in_specs=mixer_specs...  34.5 us
    unnamed x100, local copies, waits for them, and re-layouts  15.4 us
    pallas_call x1, Pallas kernels, local(): pl.pallas_call(forward_kernel, grid=(seqs, groups), in_specs=mixer_specs,...  14.9 us
  transfers between devices with their start and end apart: 6, of which 2 were waited for; matrix products, arithmetic and copies ran while one was open for 22% of the time, Pallas kernels for 31%

profile of v1, /device:TPU:0, one launch (start us, length us, event | category | flops | bytes accessed | tf_op | source)
XLA Modules:
  0.0 517.2 jit_solution(12660352224739127761)
XLA Ops:
  14.8 79.6 %all-gather.3.cloned.1.call-done = bf16[1024,4384]{1,0:T(8,128)(2,1)} async-done(((bf16[32,4384]{1,0:T(8,128)(2,1)}), bf16[1024,4384]{1,0:T(8,128)(2,1)}) %all-gather.3.cloned.1.call-update) | async-done | bytes 8978448 | tf_op jit(solution)/shard_map/all_gather | solution.py:384
  94.4 13.9 %fusion.38 = (bf16[512,4384]{0,1:T(8,128)(2,1)}, f32[512,4384]{0,1:T(8,128)}) fusion(bf16[512,1024]{1,0:T(8,128)(2,1)S(1)} %bitcast.99, bf16[1024,4384]{1,0:T(8,128)(2,1)} %all-gather.3.cloned.1.call-done), kind=kOutput, calls=%fused_computation.83 | convolution fusion | flops 4599201792 | bytes 23494656 | tf_op jit(solution)/shard_map/dot_general | solution.py:389
  108.3 6.5 %copy.82 = bf16[512,4384]{1,0:T(8,128)(2,1)} copy(bf16[512,4384]{0,1:T(8,128)(2,1)} %get-tuple-element.127) | data formatting | bytes 8978432 | tf_op jit(solution)/shard_map/convert.8
  115.8 2.2 collective-permute-start
  122.4 9.8 %copy.90.x_ref.gate_ref = f32[512,4384]{1,0:T(8,128)} copy(f32[512,4384]{0,1:T(8,128)} %get-tuple-element.128) | data formatting | bytes 17956864 | tf_op jit(solution)/shard_map/dot_general | solution.py:389
  133.5 14.9 %mixer_forward.1 = (f32[4,128,2048]{2,1,0:T(8,128)S(1)}, f32[4,128,2048]{2,1,0:T(8,128)S(1)}, f32[4,1,2048]{2,1,0:T(1,128)S(1)}) custom-call(f32[512,4384]{1,0:T(8,128)} %copy.90.x_ref.gate_ref, bf16[4,8,2048]{2,1,0:T(8,128)(2,1)S(1)} %pad.28.halo_ref, f32[4,2304]{1,0:T(4,128)S(1)} %copy-done.8, f32[1,2304]{1,0:T(1,128)S(1)} %broadcast_in_dim.49.bias_ref, ...), custom_call_target="tpu_custom_call" | custom-call | tf_op jit(solution)/shard_map/mixer_forward/pallas_call | solution.py:434
  148.5 5.7 %chain_up.1.start_ref = bf16[4,128,2048]{2,1,0:T(8,128)(2,1)S(1)} custom-call(f32[4,128,2048]{2,1,0:T(8,128)S(1)} %get-tuple-element.29.local_ref, f32[4,1,2048]{2,1,0:T(1,128)S(1)} %get-tuple-element.30.dec_ref), custom_call_target="tpu_custom_call" | custom-call | tf_op jit(solution)/shard_map/chain_up/pallas_call | solution.py:84
  154.2 10.9 %mixer_finish.1 = (bf16[512,2048]{1,0:T(8,128)(2,1)S(1)}, bf16[512,2048]{1,0:T(8,128)(2,1)S(1)}) custom-call(f32[4,128,2048]{2,1,0:T(8,128)S(1)} %get-tuple-element.28.y_ref, bf16[4,128,2048]{2,1,0:T(8,128)(2,1)S(1)} %chain_up.1.start_ref, f32[4,128,256]{2,1,0:T(8,128)S(1)} %get-tuple-element.106.b_ref.c_ref, f32[4,128,32]{2,1,0:T(8,128)S(1)} %bitcast.78, ...), custom_call_target="tpu_custom_call" | custom-call | tf_op jit(solution)/shard_map/mixer_finish/pallas_call | solution.py:458
  167.8 4.4 convert_bitcast_fusion
  172.2 6.6 %copy.116 = bf16[1024,2048]{1,0:T(8,128)(2,1)} copy(bf16[1024,2048]{0,1:T(8,128)(2,1)} %convert_bitcast_fusion) | data formatting | bytes 8388608
  179.4 7.0 %fusion.40.grad_ref = f32[512,2048]{1,0:T(8,128)} fusion(bf16[512,1024]{1,0:T(8,128)(2,1)} %bitcast.100, bf16[1024,2048]{1,0:T(8,128)(2,1)} %all-gather.5.cloned.1.call-done), kind=kOutput, calls=%fused_computation.85 | convolution fusion | flops 2147483648 | bytes 9437184 | tf_op jit(solution)/shard_map/dot_general | solution.py:115
  186.5 9.2 %post_backward.1 = (bf16[512,2048]{1,0:T(8,128)(2,1)S(1)}, bf16[512,2048]{1,0:T(8,128)(2,1)S(1)}, f32[1,2048]{1,0:T(1,128)S(1)}, f32[4,128,2048]{2,1,0:T(8,128)S(1)}) custom-call(f32[512,2048]{1,0:T(8,128)} %fusion.40.grad_ref, bf16[512,2048]{1,0:T(8,128)(2,1)S(1)} %copy-done.5, f32[512,4384]{1,0:T(8,128)} %copy.90.x_ref.gate_ref, f32[1,2048]{1,0:T(1,128)S(1)} %bitcast.87, ...), custom_call_target="tpu_custom_call" | custom-call | tf_op jit(solution)/shard_map/post_backward/pallas_call | solution.py:474
  195.7 86.1 %chain_down.1.right_ref = bf16[4,128,2048]{2,1,0:T(8,128)(2,1)S(1)} custom-call(f32[4,128,2048]{2,1,0:T(8,128)S(1)} %get-tuple-element.35.local_ref, f32[4,1,2048]{2,1,0:T(1,128)S(1)} %get-tuple-element.30.dec_ref), custom_call_target="tpu_custom_call" | custom-call | tf_op jit(solution)/shard_map/chain_down/pallas_call | solution.py:84
  281.8 34.5 %mixer_backward.1 = (f32[512,2048]{1,0:T(8,128)}, f32[4,8,2048]{2,1,0:T(8,128)S(1)}, f32[4,8,2048]{2,1,0:T(8,128)S(1)}, f32[4,4,128,8]{3,2,1,0:T(8,128)S(1)}, f3...) custom-call(f32[512,4384]{1,0:T(8,128)} %copy.90.x_ref.gate_ref, ...), custom_call_target="tpu_custom_call" | custom-call | tf_op jit(solution)/shard_map/mixer_backward/pallas_call | solution.py:489
  321.4 1.5 copy.98
  331.1 2.4 fusion.33
  333.6 2.6 slice.201
  337.5 10.2 %bitcast_convert_fusion = bf16[1024,4384]{1,0:T(8,128)(2,1)} fusion(bf16[4,128,1024]{2,1,0:T(8,128)(2,1)S(1)} %copy-done.24, bf16[4,128,32]{2,1,0:T(8,128)(2,1)S(1)} %get-tuple-element.104, bf16[4,3,256]{2,1,0:T(4,128)(2,1)S(1)} %fusion.30, bf16[4,125,256]{2,1,0:T(8,128)(2,1)S(1)} %slice.202, bf16[4,3,2048]{2,1,0:T(4,128)(2,1)S(1)} %fusion.22, ...), kind=kOutput, calls=%fused_computation | convolution fusion | flops 4628381696 | bytes 14516224 | tf_op jit(solution)/shard_map/dot_general | solution.py:115
  349.5 6.1 %fusion.39 = f32[512,1024]{1,0:T(8,128)} fusion(bf16[512,2048]{1,0:T(8,128)(2,1)S(1)} %copy-done.12, bf16[1024,2048]{1,0:T(8,128)(2,1)} %all-gather.5.cloned.1.call-done), kind=kOutput, calls=%fused_computation.84 | convolution fusion | flops 2147483648 | bytes 8388608 | tf_op jit(solution)/shard_map/dot_general | solution.py:115
  355.6 10.9 %fusion.5 = (f32[1024]{0:T(1024)S(1)}, f32[4,128]{1,0:T(4,128)}, f32[4,128,1024]{2,1,0:T(8,128)}) fusion(bf16[4,128,1024]{2,1,0:T(8,128)(2,1)S(1)} %copy-done.18, f32[4,128]{1,0:T(4,128)S(1)} %fusion.31, f32[1024]{0:T(1024)S(1)} %copy-done.32, bf16[1024,4384]{1,0:T(8,128)(2,1)} %all-gather.3.cloned.1.call-done, bf16[4,128,32]{2,1,0:T(8,128)(2,1)S(1)} %copy-done.47, ...), kind=kOutput, calls=%fused_computation.15 | convolution fusion | flops 4627560960 | bytes 16625664 | tf_op jit(solution)/shard_map/dot_general | solution.py:115
  366.6 42.3 %all-reduce.9 = (f32[1024]{0:T(1024)}, f32[4,2304]{1,0:T(4,128)}, f32[2304]{0:T(1024)}, f32[32]{0:T(128)}, f32[32]{0:T(128)}, /*index=5*/f32[32]{0:T(128)}, f32[2048]{0:T(1024)}) all-reduce(f32[1024]{0:T(1024)S(1)} %get-tuple-element.89, f32[4,2304]{1,0:T(4,128)S(1)} %pad_maximum_fusion.2, ...), channel_id=1, replica_groups=mesh['batch'=4,'seq'=8] {'batch','seq'}, use_global_device_ids=true, to_apply=%region_4.5 | all-reduce | flops 14688 | bytes 117504 | tf_op jit(solution)/shard_map/psum | solution.py:563
  409.6 4.3 fusion.6
  416.0 92.9 %reduce-scatter.5.cloned.1.call-done = bf16[32,4384]{1,0:T(8,128)(2,1)} async-done(((bf16[1024,4384]{1,0:T(8,128)(2,1)}), bf16[32,4384]{1,0:T(8,128)(2,1)}) %reduce-scatter.5.cloned.1.call-update) | async-done | bytes 280592 | tf_op jit(solution)/shard_map/reduce_scatter | solution.py:557
  508.9 1.8 convert_element_type.56
  (163 shorter events, 36.3 us)
Async XLA Ops:
  7.2 87.2 %all-gather.3.cloned.1.call-start = ((), (), s32[]{:S(2)}) async-start(), calls=%async_computation.2 | async-start | bytes 9461760 | tf_op jit(solution)/shard_map/all_gather | solution.py:384
  7.9 171.5 %all-gather.5.cloned.1.call-start = ((), (), s32[]{:S(2)}) async-start(), calls=%async_computation.3 | async-start | bytes 4325376 | tf_op jit(solution)/shard_map/all_gather | solution.py:385
  8.7 405.3 %reduce-scatter.7.cloned.1.call-start = ((), (), s32[]{:S(2)}) async-start(), calls=%async_computation.5 | async-start | bytes 4325376
  12.4 106.7 %copy-start.43 = (f32[32]{0:T(128)}, f32[32]{0:T(128)S(1)}, u32[]{:S(2)}) copy-start(f32[32]{0:T(128)S(1)} %exponential_negate_fusion) | copy-start | bytes 388
  13.3 119.1 %copy-start.33 = (f32[1,256]{1,0:T(1,128)}, f32[1,256]{1,0:T(1,128)S(1)}, u32[]{:S(2)}) copy-start(f32[1,256]{1,0:T(1,128)S(1)} %get-tuple-element.125) | copy-start | bytes 3076
  13.3 119.1 %copy-start.34 = (f32[1,256]{1,0:T(1,128)}, f32[1,256]{1,0:T(1,128)S(1)}, u32[]{:S(2)}) copy-start(f32[1,256]{1,0:T(1,128)S(1)} %get-tuple-element.126) | copy-start | bytes 3076
  14.8 93.5 %copy-start.23 = (bf16[4,128,1024]{2,1,0:T(8,128)(2,1)}, bf16[4,128,1024]{2,1,0:T(8,128)(2,1)S(1)}, u32[]{:S(2)}) copy-start(bf16[4,128,1024]{2,1,0:T(8,128)(2,1)S(1)} %fusion.4) | copy-start | bytes 3145732
  108.3 9.7 %copy-start.40 = (f32[32]{0:T(128)S(1)}, f32[32]{0:T(128)}, u32[]{:S(2)}) copy-start(f32[32]{0:T(128)} %param.17) | copy-start | bytes 388
  115.8 16.4 %collective-permute-start = (bf16[4,3,2304]{2,1,0:T(4,128)(2,1)S(1)}, bf16[4,3,2304]{2,1,0:T(4,128)(2,1)S(1)}, u32[]{:S(2)}, u32[]{:S(2)}) collective-permute-start(bf16[4,3,2304]{2,1,0:T(4,128)(2,1)S(1)} %slice.149), channel_id=1, source_target_pairs={{0,1},{1,2},{2,3},{3,4},{4,5},{5,6},{6,7},{8,9},{9,10},{10,11},{11... | collective-permute-start | bytes 165896 | tf_op jit(solution)/shard_map/ppermute | solution.py:391
  122.0 11.5 %copy-start = (f32[4,128,4,8]{3,1,2,0:T(8,128)}, f32[4,128,4,8]{3,1,2,0:T(8,128)S(1)}, u32[]{:S(2)}) copy-start(f32[4,128,4,8]{3,1,2,0:T(8,128)S(1)} %copy.84) | copy-start | bytes 196612
  122.3 11.2 %copy-start.2 = (f32[4,128,4,8]{3,1,2,0:T(8,128)}, f32[4,128,4,8]{3,1,2,0:T(8,128)S(1)}, u32[]{:S(2)}) copy-start(f32[4,128,4,8]{3,1,2,0:T(8,128)S(1)} %copy.89) | copy-start | bytes 196612
  122.4 10.0 %slice-start = ((f32[2304]{0:T(1024)}), f32[256]{0:T(256)S(1)}, s32[]{:S(2)}) async-start(f32[2304]{0:T(1024)} %param.16), calls=%async_computation.6 | async-start | bytes 2048 | tf_op jit(solution)/shard_map/slice | solution.py:397
  154.2 13.6 %copy-start.25 = (bf16[4,128,1024]{2,1,0:T(8,128)(2,1)S(1)}, bf16[4,128,1024]{2,1,0:T(8,128)(2,1)}, u32[]{:S(2)}) copy-start(bf16[4,128,1024]{2,1,0:T(8,128)(2,1)} %param.12) | copy-start | bytes 3145732
  178.8 330.1 %reduce-scatter.5.cloned.1.call-start = ((), (), s32[]{:S(2)}) async-start(), calls=%async_computation.4 | async-start | bytes 9461760 | tf_op jit(solution)/shard_map/reduce_scatter | solution.py:557
  179.4 7.0 %copy-start.5 = (bf16[512,2048]{1,0:T(8,128)(2,1)S(1)}, bf16[512,2048]{1,0:T(8,128)(2,1)}, u32[]{:S(2)}) copy-start(bf16[512,2048]{1,0:T(8,128)(2,1)} %copy-done.4) | copy-start | bytes 6291460
  195.7 120.6 %copy-start.13 = (bf16[512,2048]{1,0:T(8,128)(2,1)}, bf16[512,2048]{1,0:T(8,128)(2,1)S(1)}, u32[]{:S(2)}) copy-start(bf16[512,2048]{1,0:T(8,128)(2,1)S(1)} %get-tuple-element.33) | copy-start | bytes 6291460
  195.7 86.1 %copy-start.1 = (f32[4,128,4,8]{3,1,2,0:T(8,128)S(1)}, f32[4,128,4,8]{3,1,2,0:T(8,128)}, u32[]{:S(2)}) copy-start(f32[4,128,4,8]{3,1,2,0:T(8,128)} %copy-done) | copy-start | bytes 196612
  195.7 86.1 %copy-start.3 = (f32[4,128,4,8]{3,1,2,0:T(8,128)S(1)}, f32[4,128,4,8]{3,1,2,0:T(8,128)}, u32[]{:S(2)}) copy-start(f32[4,128,4,8]{3,1,2,0:T(8,128)} %copy-done.2) | copy-start | bytes 196612
  319.0 7.5 %copy-start.17 = (f32[4,131,256]{2,1,0:T(8,128)S(1)}, f32[4,131,256]{2,1,0:T(8,128)}, u32[]{:S(2)}) copy-start(f32[4,131,256]{2,1,0:T(8,128)} %copy-done.16) | copy-start | bytes 1609732
  319.0 7.5 %copy-start.21 = (f32[4,128,256]{2,1,0:T(8,128)S(1)}, f32[4,128,256]{2,1,0:T(8,128)}, u32[]{:S(2)}) copy-start(f32[4,128,256]{2,1,0:T(8,128)} %get-tuple-element.107) | copy-start | bytes 1572868
  329.5 6.8 %collective-permute-start.1 = (f32[4,3,2304]{2,1,0:T(4,128)}, f32[4,3,2304]{2,1,0:T(4,128)S(1)}, u32[]{:S(2)}, u32[]{:S(2)}) collective-permute-start(f32[4,3,2304]{2,1,0:T(4,128)} %pad_maximum_fusion.1), channel_id=1, source_target_pairs={{1,0},{2,1},{3,2},{4,3},{5,4},{6,5},{7,6},{9,8},{10,9},{11,10},{12... | collective-permute-start | bytes 331784 | tf_op jit(solution)/shard_map/ppermute | solution.py:541
  331.1 6.4 %copy-start.14 = (bf16[512,2048]{1,0:T(8,128)(2,1)S(1)}, bf16[512,2048]{1,0:T(8,128)(2,1)}, u32[]{:S(2)}) copy-start(bf16[512,2048]{1,0:T(8,128)(2,1)} %copy-done.13) | copy-start | bytes 6291460
  333.6 14.2 %copy-start.27 = (bf16[4,125,256]{2,1,0:T(8,128)(2,1)}, bf16[4,125,256]{2,1,0:T(8,128)(2,1)S(1)}, u32[]{:S(2)}) copy-start(bf16[4,125,256]{2,1,0:T(8,128)(2,1)S(1)} %slice.202) | copy-start | bytes 768004
  355.6 54.0 %copy-start.22 = (f32[512,1024]{1,0:T(8,128)S(1)}, f32[512,1024]{1,0:T(8,128)}, u32[]{:S(2)}) copy-start(f32[512,1024]{1,0:T(8,128)} %fusion.39) | copy-start | bytes 6291460
  (31 other events, 91.7 us)
Sparse Core Ops, SparseCore 0:
  10.9 83.4 all-gather.2
  97.4 60.7 all-gather.4
  178.9 176.4 reduce-scatter.6
  357.6 151.2 reduce-scatter.4

commit v2 on v1

--- a/solution.py
+++ b/solution.py
@@ -131,7 +131,7 @@
 def conv_pre(x_ref, halo_ref, taps_ref, bias_ref, ext):
     length = x_ref.shape[0]
     ext[0:8, :] = halo_ref[0].astype(F32)
-    ext[8 : 8 + length, :] = x_ref[...].astype(BF).astype(F32)
+    ext[8 : 8 + length, :] = x_ref[...].astype(F32)
     pre = bias_ref[...]
     for k in range(CONV):
         pre = pre + taps_ref[k : k + 1, :] * ext[5 + k : 5 + k + length, :]
@@ -241,7 +241,7 @@
 def backward_kernel(
     x_ref, halo_ref, taps_ref, bias_ref, b_ref, c_ref, step_ref, cum_ref, cumt_ref, skip_ref,
     dy_ref, right_ref, start_ref,
-    back_ref, head_ref, stats_ref, dstep_ref, dcum_ref, dcumt_ref, db_ref, dc_ref, ext, late,
+    back_ref, head_ref, edge_ref, stats_ref, dstep_ref, dcum_ref, dcumt_ref, db_ref, dc_ref, ext, late,
 ):
     pre = conv_pre(x_ref, halo_ref, taps_ref, bias_ref, ext)
     length = pre.shape[0]
@@ -328,8 +328,182 @@
     total = taps_ref[0:1, :] * late[HALO : HALO + length, :]
     for k in range(1, CONV):
         total = total + taps_ref[k : k + 1, :] * late[HALO - k : HALO - k + length, :]
-    back_ref[...] = total
+    back_ref[...] = total.astype(BF)
+    edge_ref[0] = total[length - 8 : length]
     head_ref[0] = late[0:8, :]
+
+
+def scatter_kernel(
+    part_ref, vec_ref, out_ref, all_ref,
+    got_a, sum_a, got_b, sum_b, got_c, vec_a, vec_b, vec_c, own_b, own_c, *sems,
+):
+    send_a, recv_a, send_b, recv_b, send_c, recv_c = sems[:6]
+    vsend_a, vrecv_a, vsend_b, vrecv_b, vsend_c, vrecv_c = sems[6:]
+    batches, size = lax.axis_size("batch"), lax.axis_size("seq")
+    pairs = size // 2
+    mine, seq = lax.axis_index("batch"), lax.axis_index("seq")
+    pair, core = seq // 2, seq % 2
+    other = pair * 2 + 1 - core
+
+    def batch_at(d):
+        return (mine + d) % batches
+
+    def pair_at(d):
+        return (pair + d) % pairs
+
+    def copy(src, dst, send, recv, batch, place):
+        return pltpu.make_async_remote_copy(
+            src_ref=src,
+            dst_ref=dst,
+            send_sem=send,
+            recv_sem=recv,
+            device_id={"batch": batch, "seq": place},
+            device_id_type=pl.DeviceIdType.MESH,
+        )
+
+    partners = [(mine, other)]
+    partners += [(batch_at(d), seq) for d in range(1, batches)]
+    partners += [(mine, pair_at(d) * 2 + core) for d in range(1, pairs)]
+    barrier = pltpu.get_barrier_semaphore()
+    for batch, place in partners:
+        pl.semaphore_signal(
+            barrier, inc=1, device_id={"batch": batch, "seq": place},
+            device_id_type=pl.DeviceIdType.MESH,
+        )
+    pl.semaphore_wait(barrier, len(partners))
+
+    def first(b):
+        return copy(
+            part_ref.at[b, :, 1 - core], got_a.at[b], send_a.at[b], recv_a.at[b], mine, other
+        )
+
+    def second(d):
+        b = batch_at(d)
+        return copy(sum_a.at[b], got_b.at[mine], send_b.at[b], recv_b.at[mine], b, seq)
+
+    def third(d):
+        p = pair_at(d)
+        return copy(
+            sum_b.at[p], got_c.at[pair], send_c.at[p], recv_c.at[pair], mine, p * 2 + core
+        )
+
+    def vec_first():
+        return copy(vec_ref, vec_a, vsend_a.at[0], vrecv_a.at[0], mine, other)
+
+    def vec_second(d, slot):
+        b = batch_at(d)
+        return copy(own_b, vec_b.at[slot], vsend_b.at[b], vrecv_b.at[slot], b, seq)
+
+    def vec_third(d, slot):
+        p = pair_at(d)
+        return copy(
+            own_c, vec_c.at[slot], vsend_c.at[p], vrecv_c.at[slot], mine, p * 2 + core
+        )
+
+    order = list(range(1, batches)) + [0]
+    vec_first().start()
+    for d in order:
+        first(batch_at(d)).start()
+    vec_first().wait_recv()
+    own_b[...] = vec_ref[...] + vec_a[...]
+    vec_b[mine] = own_b[...]
+    for d in range(1, batches):
+        vec_second(d, mine).start()
+    for d in order:
+        b = batch_at(d)
+        first(b).wait_recv()
+
+        def add_a(p, carry):
+            sum_a[b, p] = (
+                part_ref[b, p, core].astype(F32) + got_a[b, p].astype(F32)
+            ).astype(BF)
+            return carry
+
+        lax.fori_loop(0, pairs, add_a, 0)
+        if d:
+            second(d).start()
+    for d in range(1, batches):
+        b = batch_at(d)
+        copy(sum_a.at[b], got_b.at[b], send_b.at[b], recv_b.at[b], b, seq).wait_recv()
+    for d in range(1, batches):
+        vec_second(d, batch_at(d)).wait_recv()
+    vec = vec_b[0]
+    for b in range(1, batches):
+        vec = vec + vec_b[b]
+    own_c[...] = vec
+    vec_c[pair] = vec
+    for d in range(1, pairs):
+        vec_third(d, pair).start()
+    for d in list(range(1, pairs)) + [0]:
+        p = pair_at(d)
+        total = sum_a[mine, p].astype(F32)
+        for e in range(1, batches):
+            total = total + got_b[batch_at(e), p].astype(F32)
+        if d:
+            sum_b[p] = total.astype(BF)
+            third(d).start()
+    for d in range(1, pairs):
+        p = pair_at(d)
+        copy(
+            sum_b.at[p], got_c.at[p], send_c.at[p], recv_c.at[p], mine, p * 2 + core
+        ).wait_recv()
+        total = total + got_c[p].astype(F32)
+    out_ref[...] = total
+    for d in range(1, pairs):
+        vec_third(d, pair_at(d)).wait_recv()
+    vec = vec_c[0]
+    for p in range(1, pairs):
+        vec = vec + vec_c[p]
+    all_ref[...] = vec
+    vec_first().wait_send()
+    for d in range(1, batches):
+        vec_second(d, mine).wait_send()
+    for d in range(1, pairs):
+        vec_third(d, pair).wait_send()
+    for d in order:
+        first(batch_at(d)).wait_send()
+    for d in range(1, batches):
+        second(d).wait_send()
+    for d in range(1, pairs):
+        third(d).wait_send()
+
+
+def scatter_sum(part, vec):
+    both = ("batch", "seq")
+    batches, size = lax.axis_size("batch"), lax.axis_size("seq")
+    total, width = part.shape
+    rows = total // (batches * size)
+    if rows % 16 or size % 2:
+        rows_sum = lax.psum_scatter(part, both, scatter_dimension=0, tiled=True)
+        return rows_sum.astype(F32), lax.psum(vec, both)
+    pairs = size // 2
+    sems = [n for n in (batches, batches, pairs, 1, batches, pairs) for _ in range(2)]
+    return pl.pallas_call(
+        scatter_kernel,
+        out_shape=[
+            jax.ShapeDtypeStruct((rows, width), F32),
+            jax.ShapeDtypeStruct(vec.shape, F32),
+        ],
+        in_specs=[pl.BlockSpec(memory_space=pltpu.VMEM)] * 2,
+        out_specs=[pl.BlockSpec(memory_space=pltpu.VMEM)] * 2,
+        scratch_shapes=[
+            pltpu.VMEM((batches, pairs, rows, width), BF),
+            pltpu.VMEM((batches, pairs, rows, width), BF),
+            pltpu.VMEM((batches, pairs, rows, width), BF),
+            pltpu.VMEM((pairs, rows, width), BF),
+            pltpu.VMEM((pairs, rows, width), BF),
+            pltpu.VMEM(vec.shape, F32),
+            pltpu.VMEM((batches,) + vec.shape, F32),
+            pltpu.VMEM((pairs,) + vec.shape, F32),
+            pltpu.VMEM(vec.shape, F32),
+            pltpu.VMEM(vec.shape, F32),
+        ]
+        + [pltpu.SemaphoreType.DMA((n,)) for n in sems],
+        compiler_params=pltpu.CompilerParams(
+            collective_id=2, has_side_effects=True, vmem_limit_bytes=48 * MIB
+        ),
+        name="scatter_sum",
+    )(part.reshape(batches, pairs, 2, rows, width), vec)
 
 
 def causal_filter(values, taps, bias):
@@ -382,20 +556,31 @@
     down = [(i + 1, i) for i in range(size - 1)]
     both = ("batch", "seq")
     inproj_full = lax.all_gather(inproj_weight, both, axis=0, tiled=True)
-    outproj_full = lax.all_gather(outproj_weight, both, axis=0, tiled=True)
+    inproj_full, outproj_later = lax.optimization_barrier((inproj_full, outproj_weight))
+    outproj_full = lax.all_gather(outproj_later, both, axis=0, tiled=True)
     token_f = tokens.astype(F32)
     normed_f, pre_back = jax.vjp(prenorm, token_f, prenorm_gain)
     normed = normed_f.astype(BF).reshape(rows, width)
-    proj = jnp.dot(normed, inproj_full, preferred_element_type=F32)
-    by_seq = proj.reshape(seqs, length, PROJ)
+    small = 2 * INNER
+    weights_gate = inproj_full[:, :INNER]
+    weights_x = inproj_full[:, INNER:small]
+    weights_rest = inproj_full[:, small:]
+    gate = mul(normed, weights_gate)
+    x_raw = mul(normed, weights_x).astype(BF)
+    rest = mul(normed, weights_rest).astype(BF).reshape(seqs, length, PROJ - small)
+    x_seq = x_raw.reshape(seqs, length, INNER)
     halo = lax.ppermute(
-        by_seq[:, length - HALO :, INNER : 2 * INNER + 2 * STATE].astype(BF), "seq", up
+        jnp.concatenate(
+            [x_seq[:, length - HALO :], rest[:, length - HALO :, : 2 * STATE]], 2
+        ),
+        "seq",
+        up,
     )
     halo_x = jnp.pad(halo[..., :INNER], ((0, 0), (8 - HALO, 0), (0, 0)))
-    bc_sent = by_seq[..., 2 * INNER : 2 * INNER + 2 * STATE].astype(BF)
+    bc_sent = rest[..., : 2 * STATE]
     bc_ext = jnp.concatenate([halo[..., INNER:], bc_sent], 1).astype(F32)
     bc_conv, bc_vjp = jax.vjp(bc_part, bc_ext, conv_taps[:, INNER:], conv_bias[INNER:])
-    step_sent = by_seq[..., 2 * INNER + 2 * STATE :].astype(BF).astype(F32)
+    step_sent = rest[..., 2 * STATE :].astype(F32)
     (step, cum), step_vjp = jax.vjp(step_part, step_sent, step_bias, decay_log)
 
     def grouped(v):
@@ -409,9 +594,8 @@
     skip = jnp.repeat(skip_weight, HEADDIM)[None, :]
     bias = conv_bias[None, :]
     gain = postnorm_gain[None, :]
-    offset = INNER // WIDE
     mixer_specs = [
-        pl.BlockSpec((length, WIDE), lambda q, g: (q, offset + g)),
+        pl.BlockSpec((length, WIDE), lambda q, g: (q, g)),
         pl.BlockSpec((1, 8, WIDE), lambda q, g: (q, 0, g)),
         pl.BlockSpec((CONV, WIDE), lambda q, g: (0, g)),
         pl.BlockSpec((1, WIDE), lambda q, g: (0, g)),
@@ -423,7 +607,7 @@
         pl.BlockSpec((1, WIDE), lambda q, g: (0, g)),
     ]
     mixer_args = (
-        proj, halo_x, conv_taps, bias, bc_conv, bc_conv, step_g, cum_g, cum_t, skip,
+        x_raw, halo_x, conv_taps, bias, bc_conv, bc_conv, step_g, cum_g, cum_t, skip,
     )
     row_block = pl.BlockSpec((length, WIDE), lambda q, g: (q, g))
     state_block = pl.BlockSpec((1, STATE, WIDE), lambda q, g: (q, 0, g))
@@ -463,13 +647,10 @@
         out_shape=[shape((rows, INNER), BF), shape((rows, INNER), BF)],
         compiler_params=params(("arbitrary",)),
         name="mixer_finish",
-    )(y_local, start, bc_conv, cum, proj, gain)
+    )(y_local, start, bc_conv, cum, gate, gain)
     branch = mul(y_norm, outproj_full, LAST)
     mixed = (token_f + branch.reshape(seqs, length, width)).astype(BF)
     upstream = cotangent.reshape(rows, width)
-    outproj_grad = lax.psum_scatter(
-        mul(upstream, y_norm, FIRST).astype(BF), both, scatter_dimension=0, tiled=True
-    ).astype(F32)
     norm_grad = mul(upstream, outproj_full)
     gate_grad, y_grad, gain_grad, state_grad = pl.pallas_call(
         post_kernel,
@@ -484,9 +665,15 @@
         ],
         compiler_params=params(("arbitrary",)),
         name="post_backward",
-    )(norm_grad, y_sent, proj, gain, bc_conv, cum)
+    )(norm_grad, y_sent, gate, gain, bc_conv, cum)
     right = run_chain(state_grad, dec, False)
-    back, head, stats, dstep, dcum, dcum_t, db, dc = pl.pallas_call(
+    right, y_late, gate_late = lax.optimization_barrier((right, y_norm, gate_grad))
+    early = jnp.concatenate(
+        [mul(upstream, y_late, FIRST).astype(BF), mul(normed, gate_late, FIRST).astype(BF)], 1
+    )
+    early = lax.psum_scatter(early, both, scatter_dimension=0, tiled=True).astype(F32)
+    outproj_grad = early[:, :INNER]
+    back, head, edge, stats, dstep, dcum, dcum_t, db, dc = pl.pallas_call(
         backward_kernel,
         grid=(seqs, groups),
         in_specs=mixer_specs + [row_block, state_block, state_block],
@@ -494,6 +681,7 @@
             row_block,
             pl.BlockSpec((1, 8, WIDE), lambda q, g: (q, 0, g)),
             pl.BlockSpec((1, 8, WIDE), lambda q, g: (q, 0, g)),
+            pl.BlockSpec((1, 8, WIDE), lambda q, g: (q, 0, g)),
             pl.BlockSpec((1, 1, length, GROUP), lambda q, g: (q, g, 0, 0)),
             pl.BlockSpec((1, 1, length, GROUP), lambda q, g: (q, g, 0, 0)),
             pl.BlockSpec((1, 1, GROUP, length), lambda q, g: (q, g, 0, 0)),
@@ -501,7 +689,8 @@
             pl.BlockSpec((1, length, STATE), lambda q, g: (q, 0, 0)),
         ],
         out_shape=[
-            shape((rows, INNER)),
+            shape((rows, INNER), BF),
+            shape((seqs, 8, INNER)),
             shape((seqs, 8, INNER)),
             shape((seqs, 8, INNER)),
             shape((seqs, groups, length, GROUP)),
@@ -539,42 +728,49 @@
         1,
     )
     tail = lax.ppermute(jnp.concatenate([head_x, bc_grad[:, :HALO]], 2), "seq", down)
-    x_back = back.reshape(seqs, length, INNER)
-    keep = length - HALO
-    proj_grad = jnp.concatenate(
+    x_edge = (edge[:, 8 - HALO :] + tail[..., :INNER]).astype(BF)
+    x_back = lax.dynamic_update_slice(
+        back.reshape(seqs, length, INNER), x_edge, (0, length - HALO, 0)
+    ).reshape(rows, INNER)
+    rest_back = jnp.concatenate(
         [
-            gate_grad.reshape(seqs, length, INNER),
-            jnp.concatenate(
-                [x_back[:, :keep], x_back[:, keep:] + tail[..., :INNER]], 1
-            ).astype(BF),
             jnp.concatenate(
                 [bc_grad[:, HALO:length], bc_grad[:, length:] + tail[..., INNER:]], 1
-            ).astype(BF),
-            step_back.astype(BF),
+            ),
+            step_back,
         ],
         2,
-    ).reshape(rows, PROJ)
-    inproj_grad = lax.psum_scatter(
-        mul(normed, proj_grad, FIRST).astype(BF), both, scatter_dimension=0, tiled=True
-    ).astype(F32)
-    normed_grad = mul(proj_grad, inproj_full, LAST)
+    ).astype(BF).reshape(rows, PROJ - small)
+    normed_grad = (
+        mul(gate_grad, weights_gate, LAST)
+        + mul(x_back, weights_x, LAST)
+        + mul(rest_back, weights_rest, LAST)
+    )
     token_grad, prenorm_part = pre_back(normed_grad.reshape(seqs, length, width))
     input_grad = cotangent.astype(F32) + token_grad
-    summed = lax.psum(
-        (prenorm_part, taps_full, bias_full, step_full, decay_full, skip_full, gain_grad[0]),
-        both,
-    )
+    vectors = (
+        prenorm_part, taps_full, bias_full, step_full, decay_full, skip_full, gain_grad[0]
+    )
+    packed = jnp.concatenate([v.reshape(-1) for v in vectors])
+    packed = jnp.pad(packed, (0, -packed.size % 1024)).reshape(8, -1)
+    late_sum, flat = scatter_sum(
+        jnp.concatenate(
+            [mul(normed, x_back, FIRST).astype(BF), mul(normed, rest_back, FIRST).astype(BF)], 1
+        ),
+        packed,
+    )
+    inproj_grad = jnp.concatenate([early[:, INNER:], late_sum], 1)
+    flat = flat.reshape(-1)
+    summed, at = [], 0
+    for v in vectors:
+        summed.append(flat[at : at + v.size].reshape(v.shape))
+        at += v.size
     return (
         mixed,
         input_grad,
         summed[0],
         inproj_grad,
-        summed[1],
-        summed[2],
-        summed[3],
-        summed[4],
-        summed[5],
-        summed[6],
+        *summed[1:],
         outproj_grad,
     )
 

time: 519 us -> 447 us (0.86)
  waiting for transfers between devices: 174 us -> 92.3 us
  Pallas kernels: 161 us -> 221 us
  blocking collectives: 42.3 us -> 0 us
  local copies, waits for them, and re-layouts: 45.5 us -> 30.8 us
    reduce_scatter x1, waiting for transfers between devices: 92.9 us -> 0.01 us  [local(): lax.psum_scatter(early, both, scatter_dimension=0, tiled=True).astype(F32)]
    pallas_call x0 -> x1, Pallas kernels: none -> 72.6 us  [scatter_sum(): pl.pallas_call(scatter_kernel, out_shape=[jax.ShapeDtypeStruct((rows, wid...]
    psum x1 -> x0, blocking collectives: 42.3 us -> none  [local(): lax.psum((prenorm_part, taps_full, bias_full, step_full, decay_full, skip...]
    dot_general x1 -> x0, matrix products: 13.9 us -> none  [local(): proj = jnp.dot(normed, inproj_full, preferred_element_type=F32)]
    dot_general x5 -> x12, matrix products: 38.7 us -> 50.6 us  [mul(): return lax.dot_general(a, b, dims, preferred_element_type=F32)]
    pallas_call x2, Pallas kernels: 91.8 us -> 81.7 us  [run_chain(): pl.pallas_call(functools.partial(chain_kernel, forward), out_shape=jax.Sh...]
    dot_general x1 -> x0, local copies, waits for them, and re-layouts: 9.79 us -> none  [local(): proj = jnp.dot(normed, inproj_full, preferred_element_type=F32)]
    concatenate x1 -> x4, other arithmetic: 0.01 us -> 9.21 us  [the longest x1 7.88 us: local(): jnp.concatenate([mul(upstream, y_late, FIRST).astype(BF), mul(normed, gat...]
  transfers between devices with their start and end apart: 6 -> 5, of which waited for: 2 -> 2; matrix products, arithmetic and copies ran while one was open for 22% -> 15% of each run, Pallas kernels for 31% -> 31%
where the time goes in v2:
time: 447 us; the launch traced here: 441 us
  Pallas kernels  221 us (49%)
  waiting for transfers between devices  92.3 us (21%)
  matrix products  52.6 us (12%)
  local copies, waits for them, and re-layouts  30.8 us (7%)
  other arithmetic  24.6 us (6%)
  between operations  15.2 us (3%)
    all_gather x1, waiting for transfers between devices, local(): inproj_full = lax.all_gather(inproj_weight, both, axis=0, tiled=True)  86.4 us
    pallas_call x2, Pallas kernels, run_chain(): pl.pallas_call(functools.partial(chain_kernel, forward), out_shape=jax.Sh...  81.7 us
    pallas_call x1, Pallas kernels, scatter_sum(): pl.pallas_call(scatter_kernel, out_shape=[jax.ShapeDtypeStruct((rows, wid...  72.6 us
    dot_general x12, matrix products, mul(): return lax.dot_general(a, b, dims, preferred_element_type=F32)  50.6 us
    pallas_call x1, Pallas kernels, local(): pl.pallas_call(backward_kernel, grid=(seqs, groups), in_specs=mixer_specs...  33.5 us
    unnamed x145, local copies, waits for them, and re-layouts  16.8 us
    pallas_call x1, Pallas kernels, local(): pl.pallas_call(forward_kernel, grid=(seqs, groups), in_specs=mixer_specs,...  12.8 us
    pallas_call x1, Pallas kernels, local(): pl.pallas_call(finish_kernel, grid=(seqs,), in_specs=[full_seq, full_seq,...  11.6 us
  transfers between devices with their start and end apart: 5, of which 2 were waited for; matrix products, arithmetic and copies ran while one was open for 15% of the time, Pallas kernels for 31%

profile of v2, /device:TPU:0, one launch (start us, length us, event | category | flops | bytes accessed | tf_op | source)
XLA Modules:
  0.0 440.6 jit_solution(5813592337834756807)
XLA Ops:
  8.0 86.4 %all-gather.3.cloned.1.call-done = bf16[1024,4384]{1,0:T(8,128)(2,1)} async-done(((bf16[32,4384]{1,0:T(8,128)(2,1)}), bf16[1024,4384]{1,0:T(8,128)(2,1)}) %all-gather.3.cloned.1.call-update) | async-done | bytes 8978448 | tf_op jit(solution)/shard_map/all_gather | solution.py:558
  100.1 2.0 convolution_convert_fusion.1
  102.4 4.7 %fusion.8.x_ref = bf16[512,2048]{1,0:T(8,128)(2,1)S(1)} fusion(bf16[512,1024]{1,0:T(8,128)(2,1)S(1)} %bitcast.115, bf16[1024,4384]{1,0:T(8,128)(2,1)} %all-gather.3.cloned.1.call-done), kind=kOutput, calls=%fused_computation.20 | convolution fusion | flops 2148532224 | bytes 7340032 | tf_op jit(solution)/shard_map/dot_general | solution.py:115
  107.2 2.2 collective-permute-start
  109.6 6.6 %fusion.2.gate_ref = f32[512,2048]{1,0:T(8,128)} fusion(bf16[512,1024]{1,0:T(8,128)(2,1)S(1)} %bitcast.116, bf16[1024,4384]{1,0:T(8,128)(2,1)} %all-gather.3.cloned.1.call-done), kind=kOutput, calls=%fused_computation.12 | convolution fusion | flops 2147483648 | bytes 9437184 | tf_op jit(solution)/shard_map/dot_general | solution.py:115
  120.0 12.8 %mixer_forward.1 = (f32[4,128,2048]{2,1,0:T(8,128)S(1)}, f32[4,128,2048]{2,1,0:T(8,128)S(1)}, f32[4,1,2048]{2,1,0:T(1,128)S(1)}) custom-call(bf16[512,2048]{1,0:T(8,128)(2,1)S(1)} %copy-done.6, bf16[4,8,2048]{2,1,0:T(8,128)(2,1)S(1)} %pad.32.halo_ref, f32[4,2304]{1,0:T(4,128)S(1)} %copy-done.16, f32[1,2304]{1,0:T(1,128)S(1)} %broadcast_in_dim.49.bias_ref, ...), custom_call_target="tpu_custom_call" | custom-call | tf_op jit(solution)/shard_map/mixer_forward/pallas_call | solution.py:618
  132.8 6.0 %chain_up.1.start_ref = bf16[4,128,2048]{2,1,0:T(8,128)(2,1)S(1)} custom-call(f32[4,128,2048]{2,1,0:T(8,128)S(1)} %get-tuple-element.38.local_ref, f32[4,1,2048]{2,1,0:T(1,128)S(1)} %get-tuple-element.39.dec_ref), custom_call_target="tpu_custom_call" | custom-call | tf_op jit(solution)/shard_map/chain_up/pallas_call | solution.py:84
  138.9 11.6 %mixer_finish.1 = (bf16[512,2048]{1,0:T(8,128)(2,1)S(1)}, bf16[512,2048]{1,0:T(8,128)(2,1)S(1)}) custom-call(f32[4,128,2048]{2,1,0:T(8,128)S(1)} %get-tuple-element.37.y_ref, bf16[4,128,2048]{2,1,0:T(8,128)(2,1)S(1)} %chain_up.1.start_ref, f32[4,128,256]{2,1,0:T(8,128)S(1)} %get-tuple-element.71.b_ref.c_ref, f32[4,128,32]{2,1,0:T(8,128)S(1)} %bitcast.94, ...), custom_call_target="tpu_custom_call" | custom-call | tf_op jit(solution)/shard_map/mixer_finish/pallas_call | solution.py:642
  153.1 5.1 %all-gather.5.cloned.1.call-done = bf16[1024,2048]{1,0:T(8,128)(2,1)} async-done(((bf16[32,2048]{1,0:T(8,128)(2,1)}), bf16[1024,2048]{1,0:T(8,128)(2,1)}) %all-gather.5.cloned.1.call-update) | async-done | bytes 4194320 | tf_op jit(solution)/shard_map/all_gather | solution.py:560
  158.2 6.9 %convolution_bitcast_fusion.grad_ref = f32[512,2048]{1,0:T(8,128)} fusion(bf16[512,1024]{1,0:T(8,128)(2,1)} %bitcast.119, bf16[1024,2048]{1,0:T(8,128)(2,1)} %all-gather.5.cloned.1.call-done), kind=kOutput, calls=%fused_computation.18 | convolution fusion | flops 2147483648 | bytes 9437184 | tf_op jit(solution)/shard_map/dot_general | solution.py:115
  165.1 9.2 %post_backward.1 = (bf16[512,2048]{1,0:T(8,128)(2,1)S(1)}, bf16[512,2048]{1,0:T(8,128)(2,1)S(1)}, f32[1,2048]{1,0:T(1,128)S(1)}, f32[4,128,2048]{2,1,0:T(8,128)S(1)}) custom-call(f32[512,2048]{1,0:T(8,128)} %convolution_bitcast_fusion.grad_ref, bf16[512,2048]{1,0:T(8,128)(2,1)S(1)} %copy-done.10, f32[512,2048]{1,0:T(8,128)} %fusion.2.gate_ref, ...), custom_call_target="tpu_custom_call" | custom-call | tf_op jit(solution)/shard_map/post_backward/pallas_call | solution.py:655
  175.7 75.6 %chain_down.1.right_ref = bf16[4,128,2048]{2,1,0:T(8,128)(2,1)S(1)} custom-call(f32[4,128,2048]{2,1,0:T(8,128)S(1)} %get-tuple-element.45.local_ref, f32[4,1,2048]{2,1,0:T(1,128)S(1)} %get-tuple-element.39.dec_ref), custom_call_target="tpu_custom_call" | custom-call | tf_op jit(solution)/shard_map/chain_down/pallas_call | solution.py:84
  251.4 4.5 %convert_bitcast_fusion = bf16[1024,2048]{1,0:T(8,128)(2,1)} fusion(bf16[512,2048]{1,0:T(8,128)(2,1)S(1)} %copy-done.24, bf16[512,1024]{1,0:T(8,128)(2,1)S(1)} %bitcast.120), kind=kOutput, calls=%fused_computation.3 | convolution fusion | flops 2149580800 | bytes 7340032 | tf_op jit(solution)/shard_map/dot_general | solution.py:115
  255.8 4.4 convolution_convert_fusion
  260.2 7.9 %pad_maximum_fusion = bf16[1024,4096]{1,0:T(8,128)(2,1)} fusion(bf16[1024,2048]{1,0:T(8,128)(2,1)} %convolution_convert_fusion, bf16[1024,2048]{1,0:T(8,128)(2,1)} %convert_bitcast_fusion), kind=kLoop, calls=%fused_computation | loop fusion | flops 16777216 | bytes 16777216 | tf_op jit(solution)/shard_map/concatenate | solution.py:671
  272.9 33.5 %mixer_backward.1 = (bf16[512,2048]{1,0:T(8,128)(2,1)S(1)}, f32[4,8,2048]{2,1,0:T(8,128)S(1)}, f32[4,8,2048]{2,1,0:T(8,128)S(1)}, f32[4,8,2048]{2,1,0:T(8,128)S(...) custom-call(bf16[512,2048]{1,0:T(8,128)(2,1)S(1)} %copy-done.7, ...), custom_call_target="tpu_custom_call" | custom-call | tf_op jit(solution)/shard_map/mixer_backward/pallas_call | solution.py:676
  312.5 2.0 multiply_add_fusion.2
  323.8 6.0 %fusion = f32[512,1024]{1,0:T(8,128)} fusion(bf16[512,2048]{1,0:T(8,128)(2,1)S(1)} %copy-done.27, bf16[1024,4384]{1,0:T(8,128)(2,1)} %all-gather.3.cloned.1.call-done), kind=kOutput, calls=%fused_computation.10 | convolution fusion | flops 2147483648 | bytes 8388608 | tf_op jit(solution)/shard_map/dot_general | solution.py:115
  329.8 3.7 fusion.59
  338.6 4.7 %fusion.4 = f32[512,1024]{1,0:T(8,128)S(1)} fusion(bf16[512,2048]{1,0:T(8,128)(2,1)S(1)} %bitcast.106, bf16[1024,4384]{1,0:T(8,128)(2,1)} %all-gather.3.cloned.1.call-done), kind=kOutput, calls=%fused_computation.14 | convolution fusion | flops 2147483648 | bytes 8388608 | tf_op jit(solution)/shard_map/dot_general | solution.py:115
  343.4 2.0 add_add_fusion.1
  346.8 3.7 bitcast_convert_fusion
  350.9 72.6 %scatter_sum.1 = (f32[32,2336]{1,0:T(8,128)S(1)}, f32[8,1920]{1,0:T(8,128)S(1)}) custom-call(bf16[4,4,2,32,2336]{4,3,2,1,0:T(8,128)(2,1)S(1)} %bitcast.88, f32[8,1920]{1,0:T(8,128)S(1)} %reshape.193.vec_ref), custom_call_target="tpu_custom_call" | custom-call | tf_op jit(solution)/shard_map/scatter_sum/pallas_call | solution.py:481
  426.6 4.6 %fusion.15 = (f32[4,128,1024]{2,1,0:T(8,128)}, bf16[4,128,1024]{2,1,0:T(8,128)(2,1)}) fusion(bf16[4,128,1024]{2,1,0:T(8,128)(2,1)} %param.11, bf16[4,128,1024]{2,1,0:T(8,128)(2,1)} %param.12, f32[4,128]{1,0:T(4,128)S(1)} %multiply_multiply_fusion, f32[1024]{0:T(1024)S(1)} %copy-done.51, f32[4,128]{1,0:T(4,128)S(1)} %fusion.48, ...), kind=kLoop, calls=%fused_computation.25 | loop fusion | flops 5242880 | bytes 9445376 | tf_op jit(solution)/shard_map/add | solution.py:750
  (229 shorter events, 46.7 us)
Async XLA Ops:
  7.2 91.8 %copy-start.34 = (bf16[4,128,1024]{2,1,0:T(8,128)(2,1)S(1)}, bf16[4,128,1024]{2,1,0:T(8,128)(2,1)}, u32[]{:S(2)}) copy-start(bf16[4,128,1024]{2,1,0:T(8,128)(2,1)} %param.11) | copy-start | bytes 3145732
  7.2 87.2 %all-gather.3.cloned.1.call-start = ((), (), s32[]{:S(2)}) async-start(), calls=%async_computation.1 | async-start | bytes 9461760 | tf_op jit(solution)/shard_map/all_gather | solution.py:558
  7.9 150.3 %all-gather.5.cloned.1.call-start = ((), (), s32[]{:S(2)}) async-start(), calls=%async_computation.2 | async-start | bytes 4325376 | tf_op jit(solution)/shard_map/all_gather | solution.py:560
  94.4 336.9 %reduce-scatter.2.cloned.1.call-start = ((), (), s32[]{:S(2)}) async-start(), calls=%async_computation.3 | async-start | bytes 8650752 | tf_op jit(solution)/shard_map/reduce_scatter | solution.py:674
  98.2 18.0 %copy-start.69 = (f32[32]{0:T(128)}, f32[32]{0:T(128)S(1)}, u32[]{:S(2)}) copy-start(f32[32]{0:T(128)S(1)} %exponential_negate_fusion) | copy-start | bytes 388
  99.0 18.8 %copy-start.54 = (f32[1,256]{1,0:T(1,128)}, f32[1,256]{1,0:T(1,128)S(1)}, u32[]{:S(2)}) copy-start(f32[1,256]{1,0:T(1,128)S(1)} %get-tuple-element.93) | copy-start | bytes 3076
  99.0 18.8 %copy-start.56 = (f32[1,256]{1,0:T(1,128)}, f32[1,256]{1,0:T(1,128)S(1)}, u32[]{:S(2)}) copy-start(f32[1,256]{1,0:T(1,128)S(1)} %get-tuple-element.94) | copy-start | bytes 3076
  99.0 18.8 %copy-start.58 = (f32[1,256]{1,0:T(1,128)}, f32[1,256]{1,0:T(1,128)S(1)}, u32[]{:S(2)}) copy-start(f32[1,256]{1,0:T(1,128)S(1)} %get-tuple-element.95) | copy-start | bytes 3076
  99.1 18.8 %copy-start.60 = (f32[1,256]{1,0:T(1,128)}, f32[1,256]{1,0:T(1,128)S(1)}, u32[]{:S(2)}) copy-start(f32[1,256]{1,0:T(1,128)S(1)} %get-tuple-element.96) | copy-start | bytes 3076
  100.1 9.5 %copy-start.39 = (bf16[4,128,1024]{2,1,0:T(8,128)(2,1)}, bf16[4,128,1024]{2,1,0:T(8,128)(2,1)S(1)}, u32[]{:S(2)}) copy-start(bf16[4,128,1024]{2,1,0:T(8,128)(2,1)S(1)} %fusion.13) | copy-start | bytes 3145732
  102.3 14.3 %copy-start.38 = (bf16[512,288]{1,0:T(8,128)(2,1)}, bf16[512,288]{1,0:T(8,128)(2,1)S(1)}, u32[]{:S(2)}) copy-start(bf16[512,288]{1,0:T(8,128)(2,1)S(1)} %copy.73) | copy-start | bytes 884740
  102.4 7.0 %copy-start.65 = (f32[32]{0:T(128)S(1)}, f32[32]{0:T(128)}, u32[]{:S(2)}) copy-start(f32[32]{0:T(128)} %param.17) | copy-start | bytes 388
  107.1 9.1 %copy-start.5 = (bf16[512,2048]{1,0:T(8,128)(2,1)}, bf16[512,2048]{1,0:T(8,128)(2,1)S(1)}, u32[]{:S(2)}) copy-start(bf16[512,2048]{1,0:T(8,128)(2,1)S(1)} %fusion.8.x_ref) | copy-start | bytes 6291460
  107.2 10.4 %collective-permute-start = (bf16[4,3,2304]{2,1,0:T(4,128)(2,1)S(1)}, bf16[4,3,2304]{2,1,0:T(4,128)(2,1)S(1)}, u32[]{:S(2)}, u32[]{:S(2)}) collective-permute-start(bf16[4,3,2304]{2,1,0:T(4,128)(2,1)S(1)} %pad_maximum_fusion.4), channel_id=1, source_target_pairs={{0,1},{1,2},{2,3},{3,4},{4,5},{5,6},{6,7},{8,9},{9,10},{10,11},{11... | collective-permute-start | bytes 165896 | tf_op jit(solution)/shard_map/ppermute | solution.py:572
  117.8 14.9 %copy-start.30 = (f32[4,131,256]{2,1,0:T(8,128)}, f32[4,131,256]{2,1,0:T(8,128)S(1)}, u32[]{:S(2)}) copy-start(f32[4,131,256]{2,1,0:T(8,128)S(1)} %maximum_convert_fusion.1) | copy-start | bytes 1609732
  138.8 11.6 %copy-start = (bf16[4,128,2048]{2,1,0:T(8,128)(2,1)}, bf16[4,128,2048]{2,1,0:T(8,128)(2,1)S(1)}, u32[]{:S(2)}) copy-start(bf16[4,128,2048]{2,1,0:T(8,128)(2,1)S(1)} %chain_up.1.start_ref) | copy-start | bytes 6291460
  158.2 6.9 %copy-start.10 = (bf16[512,2048]{1,0:T(8,128)(2,1)S(1)}, bf16[512,2048]{1,0:T(8,128)(2,1)}, u32[]{:S(2)}) copy-start(bf16[512,2048]{1,0:T(8,128)(2,1)} %copy-done.9) | copy-start | bytes 6291460
  175.7 80.2 %copy-start.26 = (bf16[512,2048]{1,0:T(8,128)(2,1)}, bf16[512,2048]{1,0:T(8,128)(2,1)S(1)}, u32[]{:S(2)}) copy-start(bf16[512,2048]{1,0:T(8,128)(2,1)S(1)} %get-tuple-element.59) | copy-start | bytes 6291460
  175.7 75.7 %copy-start.24 = (bf16[512,2048]{1,0:T(8,128)(2,1)S(1)}, bf16[512,2048]{1,0:T(8,128)(2,1)}, u32[]{:S(2)}) copy-start(bf16[512,2048]{1,0:T(8,128)(2,1)} %copy-done.23) | copy-start | bytes 6291460
  175.7 75.7 %copy-start.44 = (bf16[4,128,1024]{2,1,0:T(8,128)(2,1)S(1)}, bf16[4,128,1024]{2,1,0:T(8,128)(2,1)}, u32[]{:S(2)}) copy-start(bf16[4,128,1024]{2,1,0:T(8,128)(2,1)} %param.12) | copy-start | bytes 3145732
  320.5 13.3 %collective-permute-start.1 = (f32[4,3,2304]{2,1,0:T(4,128)S(1)}, f32[4,3,2304]{2,1,0:T(4,128)S(1)}, u32[]{:S(2)}, u32[]{:S(2)}) collective-permute-start(f32[4,3,2304]{2,1,0:T(4,128)S(1)} %pad_maximum_fusion.3), channel_id=1, source_target_pairs={{1,0},{2,1},{3,2},{4,3},{5,4},{6,5},{7,6},{9,8},{10,9},{11,10},{12... | collective-permute-start | bytes 331784 | tf_op jit(solution)/shard_map/ppermute | solution.py:730
  323.7 10.2 %copy-start.47 = (bf16[4,128,32]{2,1,0:T(8,128)(2,1)}, bf16[4,128,32]{2,1,0:T(8,128)(2,1)S(1)}, u32[]{:S(2)}) copy-start(bf16[4,128,32]{2,1,0:T(8,128)(2,1)S(1)} %get-tuple-element.69) | copy-start | bytes 98308
  350.9 75.7 %copy-start.53 = (f32[4,128]{1,0:T(4,128)S(1)}, f32[4,128]{1,0:T(4,128)}, u32[]{:S(2)}) copy-start(f32[4,128]{1,0:T(4,128)} %copy-done.52) | copy-start | bytes 6148
  350.9 75.7 %copy-start.33 = (f32[512,1024]{1,0:T(8,128)S(1)}, f32[512,1024]{1,0:T(8,128)}, u32[]{:S(2)}) copy-start(f32[512,1024]{1,0:T(8,128)} %copy-done.32) | copy-start | bytes 6291460
  (55 other events, 140.6 us)
Sparse Core Ops, SparseCore 0:
  10.9 83.4 all-gather.2
  97.4 60.7 all-gather.4
  268.3 153.8 reduce-scatter.1
